TPU v7x, 32 devices: a whole 2x2x4 slice. The times are simulated.
32 devices in a mesh: fsdp: 32 (over z, y, x, core).
Axes of the slice: x: 2, y: 2, z: 4, core: 2. Of those that a mesh axis runs over, the one named last changes fastest.
Arguments:
- tokens: bfloat16 [64, 128, 1024], P('fsdp'), may hold values from -6 to 6
- segment_ids: int32 [64, 128], P('fsdp'), may hold values from 0 to 3, never falling along the last dimension, each value on 1 to 64 neighbouring positions
- variate_ids: int32 [64, 128], P('fsdp'), may hold values from 0 to 3
- time_ids: int32 [64, 128], P('fsdp'), may hold values from 0 to 127
- w_query: bfloat16 [1024, 1024], P('fsdp'), may hold values from -0.1875 to 0.1875
- w_key: bfloat16 [1024, 1024], P('fsdp'), may hold values from -0.1875 to 0.1875
- w_value: bfloat16 [1024, 1024], P('fsdp'), may hold values from -0.1875 to 0.1875
- w_out: bfloat16 [1024, 1024], P('fsdp'), may hold values from -0.5 to 0.5
- w_gate: bfloat16 [1024, 4096], P('fsdp'), may hold values from -0.1875 to 0.1875
- w_up: bfloat16 [1024, 4096], P('fsdp'), may hold values from -0.1875 to 0.1875
- w_down: bfloat16 [4096, 1024], P('fsdp'), may hold values from -0.09375 to 0.09375
- gain_attn: bfloat16 [1024], P('fsdp'), may hold values from 0.5 to 1.5
- gain_ffn: bfloat16 [1024], P('fsdp'), may hold values from 0.5 to 1.5
- gain_query: bfloat16 [64], replicated, may hold values from 0.099609375 to 1.8984375
- gain_key: bfloat16 [64], replicated, may hold values from 0.099609375 to 1.8984375
- variate_bias: bfloat16 [2, 16], replicated, may hold values from -3 to 3
- cotangent: bfloat16 [64, 128, 1024], P('fsdp'), may hold values from -6 to 6
Outputs:
- activations: bfloat16 [64, 128, 1024], P('fsdp')
- input_grad: bfloat16 [64, 128, 1024], P('fsdp')
- grad_query: float32 [1024, 1024], P('fsdp')
- grad_key: float32 [1024, 1024], P('fsdp')
- grad_value: float32 [1024, 1024], P('fsdp')
- grad_out: float32 [1024, 1024], P('fsdp')
- grad_gate: float32 [1024, 4096], P('fsdp')
- grad_up: float32 [1024, 4096], P('fsdp')
- grad_down: float32 [4096, 1024], P('fsdp')
- grad_gain_attn: float32 [1024], P('fsdp')
- grad_gain_ffn: float32 [1024], P('fsdp')
- grad_gain_query: float32 [64], replicated
- grad_gain_key: float32 [64], replicated
- grad_variate_bias: float32 [2, 16], replicated
Inputs may be any that keep to these rules, and one draw needn't show every extreme that they name: `segment_ids`: 0 marks padding; each other value is one document; values never fall along a sequence.
All inputs are finite; a program needn't handle non-finite values.
Results may differ from a plain program's by a relative error of at most 0.014.
The roundings to bfloat16 on the way count: a program that leaves them out, or rounds other values in their place, can miss the bound.
Values may be sent and summed in bfloat16 or wider, within the bound.
A program may use at most 384 MiB of HBM per device.

v0:
```python
import math

import jax
import jax.numpy as jnp
from jax import lax
from jax.sharding import PartitionSpec as P

EPSILON = 1e-05


def normalize(values, scale_gain):
    return (
        values * lax.rsqrt(jnp.mean(values * values, axis=-1, keepdims=True) + EPSILON) * scale_gain
    )


def rotate(values, moments):
    halfway = values.shape[-1] // 2
    frequency = jnp.exp(-math.log(10000.0) * jnp.arange(halfway).astype(jnp.float32) / halfway)
    angles = moments.astype(jnp.float32)[:, None] * frequency[None, :]
    cosine = jnp.cos(angles)[:, None, :]
    sine_part = jnp.sin(angles)[:, None, :]
    former = values[..., :halfway]
    latter = values[..., halfway:]
    return jnp.concatenate(
        [former * cosine - latter * sine_part, former * sine_part + latter * cosine], axis=-1
    )


def prepare(raw_heads, head_gain, moments, factor):
    return rotate(normalize(raw_heads, head_gain), moments) * factor


def swiglu(gate_act, up_act):
    return jax.nn.silu(gate_act) * up_act


def attention_masks(segments, variates):
    length = segments.shape[0]
    diagonal = jnp.arange(length)[:, None] == jnp.arange(length)[None, :]
    allowed = (segments[:, None] == segments[None, :]) & ((segments[None, :] != 0) | diagonal)
    same_var = variates[:, None] == variates[None, :]
    return (allowed, same_var)


def scoring(q_rot, k_rot, bias_table, allowed, same_var):
    scores = jnp.einsum("qhe,khe->hqk", q_rot, k_rot, preferred_element_type=jnp.float32)
    scores = scores + jnp.where(
        same_var[None], bias_table[1][:, None, None], bias_table[0][:, None, None]
    )
    return jnp.where(allowed[None], scores, -1000000000.0)


def project(left, right):
    return jnp.dot(left, right, preferred_element_type=jnp.float32)


def across(left, right):
    return lax.dot_general(
        left, right, (((0,), (0,)), ((), ())), preferred_element_type=jnp.float32
    )


def against(left, weight):
    return lax.dot_general(
        left, weight, (((1,), (1,)), ((), ())), preferred_element_type=jnp.float32
    )


def forward(inputs_low, weights, side_params, segments, variates, moments):
    w_query, w_key, w_value, w_out, w_gate, w_up, w_down, gain_attn, gain_ffn = weights
    gain_query, gain_key, bias_table = side_params
    length, model_width = inputs_low.shape
    head_count = bias_table.shape[1]
    head_dim = gain_query.shape[0]
    inputs = inputs_low.astype(jnp.float32)
    normed = normalize(inputs, gain_attn.astype(jnp.float32)).astype(jnp.bfloat16)
    queries = project(normed, w_query).reshape(length, head_count, head_dim)
    key_raw = project(normed, w_key).reshape(length, head_count, head_dim)
    v_low = project(normed, w_value).reshape(length, head_count, head_dim).astype(jnp.bfloat16)
    q_rot = prepare(queries, gain_query, moments, head_dim ** (-0.5)).astype(jnp.bfloat16)
    k_rot = prepare(key_raw, gain_key, moments, 1.0).astype(jnp.bfloat16)
    allowed, same_var = attention_masks(segments, variates)
    scores = scoring(q_rot, k_rot, bias_table, allowed, same_var)
    maximum = jnp.max(scores, axis=-1, keepdims=True)
    exponent = jnp.exp(scores - maximum)
    row_total = jnp.sum(exponent, axis=-1, keepdims=True)
    log_total = maximum + jnp.log(row_total)
    softmax_probs = (exponent / row_total).astype(jnp.bfloat16)
    attended = jnp.einsum("hqk,khe->qhe", softmax_probs, v_low, preferred_element_type=jnp.float32)
    attended = attended.reshape(length, model_width).astype(jnp.bfloat16)
    mixed_state = inputs + project(attended, w_out)
    normed_ffn = normalize(mixed_state, gain_ffn.astype(jnp.float32)).astype(jnp.bfloat16)
    gate_act = project(normed_ffn, w_gate)
    up_act = project(normed_ffn, w_up)
    hidden = swiglu(gate_act, up_act).astype(jnp.bfloat16)
    result = mixed_state + project(hidden, w_down)
    kept_state = (
        inputs,
        normed,
        queries,
        key_raw,
        q_rot,
        k_rot,
        v_low,
        log_total,
        attended,
        mixed_state,
        normed_ffn,
        gate_act,
        up_act,
        hidden,
    )
    return (result, kept_state)


def backward(upstream, kept_state, weights, side_params, segments, variates, moments):
    (
        inputs,
        normed,
        queries,
        key_raw,
        q_rot,
        k_rot,
        v_low,
        log_total,
        attended,
        mixed_state,
        normed_ffn,
        gate_act,
        up_act,
        hidden,
    ) = kept_state
    w_query, w_key, w_value, w_out, w_gate, w_up, w_down, gain_attn, gain_ffn = weights
    gain_query, gain_key, bias_table = side_params
    length, head_count, head_dim = queries.shape
    grad_down = across(hidden, upstream)
    d_hidden = against(upstream, w_down)
    _, pullback = jax.vjp(swiglu, gate_act, up_act)
    d_gate, d_up = pullback(d_hidden)
    d_gate = d_gate.astype(jnp.bfloat16)
    d_up = d_up.astype(jnp.bfloat16)
    grad_gate = across(normed_ffn, d_gate)
    grad_up = across(normed_ffn, d_up)
    d_normed_ffn = against(d_gate, w_gate) + against(d_up, w_up)
    _, pullback = jax.vjp(normalize, mixed_state, gain_ffn.astype(jnp.float32))
    d_mixed, grad_gain_ffn = pullback(d_normed_ffn)
    d_mixed = d_mixed + upstream.astype(jnp.float32)
    d_branch = d_mixed.astype(jnp.bfloat16)
    grad_out = across(attended, d_branch)
    d_attended = against(d_branch, w_out).astype(jnp.bfloat16).reshape(length, head_count, head_dim)
    allowed, same_var = attention_masks(segments, variates)
    scores = scoring(q_rot, k_rot, bias_table, allowed, same_var)
    softmax_probs = jnp.exp(scores - log_total)
    d_probs = jnp.einsum("qhe,khe->hqk", d_attended, v_low, preferred_element_type=jnp.float32)
    d_values = jnp.einsum(
        "hqk,qhe->khe",
        softmax_probs.astype(jnp.bfloat16),
        d_attended,
        preferred_element_type=jnp.float32,
    )
    d_values = d_values.reshape(length, head_count * head_dim).astype(jnp.bfloat16)
    weighted = jnp.sum(softmax_probs * d_probs, axis=-1, keepdims=True)
    d_scores = (softmax_probs * (d_probs - weighted)).astype(jnp.bfloat16)
    d_float = d_scores.astype(jnp.float32)
    same_sum = jnp.sum(jnp.where(same_var[None], d_float, 0.0), axis=(1, 2))
    other_sum = jnp.sum(jnp.where(same_var[None], 0.0, d_float), axis=(1, 2))
    grad_bias = jnp.stack([other_sum, same_sum])
    d_qrot = jnp.einsum("hqk,khe->qhe", d_scores, k_rot, preferred_element_type=jnp.float32)
    d_krot = jnp.einsum("hqk,qhe->khe", d_scores, q_rot, preferred_element_type=jnp.float32)
    factor = head_dim ** (-0.5)
    _, pullback = jax.vjp(
        lambda raw_heads, head_gain: prepare(raw_heads, head_gain, moments, factor),
        queries,
        gain_query,
    )
    d_queries, grad_gain_query = pullback(d_qrot)
    _, pullback = jax.vjp(
        lambda raw_heads, head_gain: prepare(raw_heads, head_gain, moments, 1.0), key_raw, gain_key
    )
    d_keys, grad_gain_key = pullback(d_krot)
    d_queries = d_queries.reshape(length, head_count * head_dim).astype(jnp.bfloat16)
    d_keys = d_keys.reshape(length, head_count * head_dim).astype(jnp.bfloat16)
    grad_query = across(normed, d_queries)
    grad_key = across(normed, d_keys)
    grad_value = across(normed, d_values)
    d_normed = against(d_queries, w_query) + against(d_keys, w_key) + against(d_values, w_value)
    _, pullback = jax.vjp(normalize, inputs, gain_attn.astype(jnp.float32))
    d_inputs, grad_gain_attn = pullback(d_normed)
    row_grads = jnp.concatenate(
        [grad_query, grad_key, grad_value, grad_out, grad_gate, grad_up], axis=1
    )
    small = (grad_gain_query, grad_gain_key, grad_bias, grad_gain_attn, grad_gain_ffn)
    return (d_inputs + d_mixed, row_grads, grad_down, small)


def local(
    tokens,
    segment_ids,
    variate_ids,
    time_ids,
    w_query,
    w_key,
    w_value,
    w_out,
    w_gate,
    w_up,
    w_down,
    gain_attn,
    gain_ffn,
    gain_query,
    gain_key,
    variate_bias,
    cotangent,
):
    devices = lax.axis_size("fsdp")
    owner = lax.axis_index("fsdp")
    width = w_query.shape[1]
    hidden_width = w_gate.shape[1]
    own_rows = w_query.shape[0]
    own_down = w_down.shape[0]
    side_params = (
        gain_query.astype(jnp.float32),
        gain_key.astype(jnp.float32),
        variate_bias.astype(jnp.float32),
    )
    rows_total = jnp.zeros((own_rows * devices, 4 * width + 2 * hidden_width), jnp.float32)
    down_total = jnp.zeros((own_down * devices, width), jnp.float32)
    side_totals = (
        jnp.zeros(gain_query.shape, jnp.float32),
        jnp.zeros(gain_key.shape, jnp.float32),
        jnp.zeros(variate_bias.shape, jnp.float32),
        jnp.zeros((own_rows * devices,), jnp.float32),
        jnp.zeros((own_rows * devices,), jnp.float32),
    )
    results = []
    input_grads = []
    for micro_index in range(tokens.shape[0]):
        segments = segment_ids[micro_index]
        variates = variate_ids[micro_index]
        moments = time_ids[micro_index]
        forward_weights = (
            lax.all_gather(w_query, "fsdp", axis=0, tiled=True),
            lax.all_gather(w_key, "fsdp", axis=0, tiled=True),
            lax.all_gather(w_value, "fsdp", axis=0, tiled=True),
            lax.all_gather(w_out, "fsdp", axis=0, tiled=True),
            lax.all_gather(w_gate, "fsdp", axis=0, tiled=True),
            lax.all_gather(w_up, "fsdp", axis=0, tiled=True),
            lax.all_gather(w_down, "fsdp", axis=0, tiled=True),
            lax.all_gather(gain_attn, "fsdp", axis=0, tiled=True),
            lax.all_gather(gain_ffn, "fsdp", axis=0, tiled=True),
        )
        result, kept_state = forward(
            tokens[micro_index], forward_weights, side_params, segments, variates, moments
        )
        results.append(result.astype(jnp.bfloat16))
        backward_weights = (
            lax.all_gather(w_query, "fsdp", axis=0, tiled=True),
            lax.all_gather(w_key, "fsdp", axis=0, tiled=True),
            lax.all_gather(w_value, "fsdp", axis=0, tiled=True),
            lax.all_gather(w_out, "fsdp", axis=0, tiled=True),
            lax.all_gather(w_gate, "fsdp", axis=0, tiled=True),
            lax.all_gather(w_up, "fsdp", axis=0, tiled=True),
            lax.all_gather(w_down, "fsdp", axis=0, tiled=True),
            lax.all_gather(gain_attn, "fsdp", axis=0, tiled=True),
            lax.all_gather(gain_ffn, "fsdp", axis=0, tiled=True),
        )
        d_inputs, row_grads, down_grads, small = backward(
            cotangent[micro_index],
            kept_state,
            backward_weights,
            side_params,
            segments,
            variates,
            moments,
        )
        input_grads.append(d_inputs.astype(jnp.bfloat16))
        rows_total = rows_total + row_grads
        down_total = down_total + down_grads
        side_totals = tuple((running + fresh for running, fresh in zip(side_totals, small)))
    owned_rows = lax.psum_scatter(rows_total, "fsdp", scatter_dimension=0, tiled=True)
    owned_down = lax.psum_scatter(down_total, "fsdp", scatter_dimension=0, tiled=True)
    shared = lax.psum(
        (side_totals[0], side_totals[1], side_totals[2], side_totals[3], side_totals[4]), "fsdp"
    )
    gain_attn_own = lax.dynamic_slice_in_dim(shared[3], owner * own_rows, own_rows, 0)
    gain_ffn_own = lax.dynamic_slice_in_dim(shared[4], owner * own_rows, own_rows, 0)
    grad_query = owned_rows[:, 0:width]
    grad_key = owned_rows[:, width : 2 * width]
    grad_value = owned_rows[:, 2 * width : 3 * width]
    grad_out = owned_rows[:, 3 * width : 4 * width]
    grad_gate = owned_rows[:, 4 * width : 4 * width + hidden_width]
    grad_up = owned_rows[:, 4 * width + hidden_width :]
    return (
        jnp.stack(results),
        jnp.stack(input_grads),
        grad_query,
        grad_key,
        grad_value,
        grad_out,
        grad_gate,
        grad_up,
        owned_down,
        gain_attn_own,
        gain_ffn_own,
        shared[0],
        shared[1],
        shared[2],
    )


def solution(mesh):
    placed = (
        P("fsdp", None, None),
        P("fsdp", None),
        P("fsdp", None),
        P("fsdp", None),
        P("fsdp", None),
        P("fsdp", None),
        P("fsdp", None),
        P("fsdp", None),
        P("fsdp", None),
        P("fsdp", None),
        P("fsdp", None),
        P("fsdp"),
        P("fsdp"),
        P(),
        P(),
        P(),
        P("fsdp", None, None),
    )
    return jax.shard_map(
        local,
        mesh=mesh,
        in_specs=placed,
        out_specs=(
            P("fsdp", None, None),
            P("fsdp", None, None),
            P("fsdp", None),
            P("fsdp", None),
            P("fsdp", None),
            P("fsdp", None),
            P("fsdp", None),
            P("fsdp", None),
            P("fsdp", None),
            P("fsdp"),
            P("fsdp"),
            P(),
            P(),
            P(),
        ),
        check_vma=False,
    )
```

profile of v0, /device:TPU:25, one launch (start us, length us, event | category | flops | bytes accessed | tf_op | source)
XLA Modules:
  0.0 1274.0 jit_solution(8898640934965833268)
XLA Ops:
  15.6 38.5 %all-reduce.11 = (bf16[1024]{0:T(1024)(128)(2,1)S(1)}, bf16[1024]{0:T(1024)(128)(2,1)S(1)}) all-reduce(bf16[1024]{0:T(1024)(128)(2,1)S(1)} %dynamic-update-slice, bf16[1024]{0:T(1024)(128)(2,1)S(1)} %dynamic-update-slice.1), channel_id=1, replica_groups=mesh['fsdp'=32] {'fsdp'}, use_global_device_ids=true, to_apply=%add.8 | all-reduce | flops 2048 | bytes 8192
  59.7 7.9 all-gather.8.cloned.1.call-done
  67.6 2.9 copy.54
  70.4 55.3 %all-gather.12.cloned.1.call-done = bf16[1024,1024]{1,0:T(8,128)(2,1)} async-done(((bf16[32,1024]{1,0:T(8,128)(2,1)}), bf16[1024,1024]{1,0:T(8,128)(2,1)}) %all-gather.12.cloned.1.call-update) | async-done | bytes 2097168 | tf_op jit(solution)/shard_map/all_gather | solution.py:244
  125.7 3.9 copy.56
  129.6 54.2 %all-gather.10.cloned.1.call-done = bf16[1024,1024]{1,0:T(8,128)(2,1)} async-done(((bf16[32,1024]{1,0:T(8,128)(2,1)}), bf16[1024,1024]{1,0:T(8,128)(2,1)}) %all-gather.10.cloned.1.call-update) | async-done | bytes 2097168 | tf_op jit(solution)/shard_map/all_gather | solution.py:243
  183.8 4.3 copy.55
  200.2 41.6 %all-gather.14.cloned.1.call-done = bf16[1024,1024]{1,0:T(8,128)(2,1)} async-done(((bf16[32,1024]{1,0:T(8,128)(2,1)}), bf16[1024,1024]{1,0:T(8,128)(2,1)}) %all-gather.14.cloned.1.call-update) | async-done | bytes 2097168 | tf_op jit(solution)/shard_map/all_gather | solution.py:246
  248.6 72.0 %all-gather.18.cloned.1.call-done = bf16[1024,4096]{1,0:T(8,128)(2,1)} async-done(((bf16[32,4096]{1,0:T(8,128)(2,1)}), bf16[1024,4096]{1,0:T(8,128)(2,1)}) %all-gather.18.cloned.1.call-update) | async-done | bytes 8388624 | tf_op jit(solution)/shard_map/all_gather | solution.py:248
  320.6 6.0 fusion.138
  326.6 72.8 %all-gather.16.cloned.1.call-done = bf16[1024,4096]{1,0:T(8,128)(2,1)} async-done(((bf16[32,4096]{1,0:T(8,128)(2,1)}), bf16[1024,4096]{1,0:T(8,128)(2,1)}) %all-gather.16.cloned.1.call-update) | async-done | bytes 8388624 | tf_op jit(solution)/shard_map/all_gather | solution.py:247
  399.4 6.0 fusion.137
  405.3 73.0 %all-gather.20.cloned.1.call-done = bf16[4096,1024]{1,0:T(8,128)(2,1)} async-done(((bf16[128,1024]{1,0:T(8,128)(2,1)}), bf16[4096,1024]{1,0:T(8,128)(2,1)}) %all-gather.20.cloned.1.call-update) | async-done | bytes 8388624 | tf_op jit(solution)/shard_map/all_gather | solution.py:249
  478.3 10.1 multiply_convert_fusion.1
  488.5 2.9 fusion.141
  491.4 7.9 multiply_reduce_fusion.7
  504.6 9.9 multiply_convert_fusion
  514.4 4.2 fusion.143
  518.9 3.5 multiply_reduce_fusion.6
  554.3 3.0 convolution_dynamic-update-slice_fusion.8
  557.3 8.2 convolution_dynamic-update-slice_fusion.3
  565.5 8.2 convolution_dynamic-update-slice_fusion.2
  584.9 8.3 convolution_dynamic-update-slice_fusion.1
  593.3 8.2 convolution_dynamic-update-slice_fusion
  601.5 49.5 %add.263 = f32[1024,12288]{1,0:T(8,128)} add(f32[1024,12288]{1,0:T(8,128)} %convolution_dynamic-update-slice_fusion.2, f32[1024,12288]{1,0:T(8,128)} %convolution_dynamic-update-slice_fusion) | non-fusion elementwise | flops 12582912 | bytes 150994944 | tf_op jit(solution)/shard_map/add | solution.py:278
  652.3 3.4 fusion.65
  655.7 11.6 convolution_add_fusion
  679.2 39.0 %all-reduce.10 = (f32[1024]{0:T(1024)S(1)}, f32[1024]{0:T(1024)S(1)}, f32[64]{0:T(128)}, f32[64]{0:T(128)}, f32[2,16]{1,0:T(2,128)}) all-reduce(f32[1024]{0:T(1024)S(1)} %add.265, f32[1024]{0:T(1024)S(1)} %add.267, f32[64]{0:T(128)S(1)} %add.268, f32[64]{0:T(128)S(1)} %add.269, ...), channel_id=1, replica_groups=mesh['fsdp'=32] {'fsdp'}, use_global_device_ids=true, to_apply=%region_26.27 | all-reduce | flops 2208 | bytes 17664 | tf_op jit(solution)/shard_map/psum | solution.py:283
  719.4 4.8 fusion.15
  724.3 4.8 fusion.14
  731.1 349.4 %reduce-scatter.3.cloned.1.call-done = f32[32,12288]{1,0:T(8,128)} async-done(((f32[1024,12288]{1,0:T(8,128)}), f32[32,12288]{1,0:T(8,128)}) %reduce-scatter.3.cloned.1.call-update) | async-done | bytes 1572880 | tf_op jit(solution)/shard_map/reduce_scatter | solution.py:281
  1084.7 182.6 %reduce-scatter.5.cloned.1.call-done = f32[128,1024]{1,0:T(8,128)} async-done(((f32[4096,1024]{1,0:T(8,128)}), f32[128,1024]{1,0:T(8,128)}) %reduce-scatter.5.cloned.1.call-update) | async-done | bytes 524304 | tf_op jit(solution)/shard_map/reduce_scatter | solution.py:282
  (408 shorter events, 100.0 us)
Async XLA Ops:
  7.2 60.4 %all-gather.8.cloned.1.call-start = ((), (), s32[]{:S(2)}) async-start(), calls=%async_computation.2 | async-start | bytes 2162688 | tf_op jit(solution)/shard_map/all_gather | solution.py:245
  7.9 117.8 %all-gather.12.cloned.1.call-start = ((), (), s32[]{:S(2)}) async-start(), calls=%async_computation.4 | async-start | bytes 2162688 | tf_op jit(solution)/shard_map/all_gather | solution.py:244
  8.7 175.2 %all-gather.10.cloned.1.call-start = ((), (), s32[]{:S(2)}) async-start(), calls=%async_computation.3 | async-start | bytes 2162688 | tf_op jit(solution)/shard_map/all_gather | solution.py:243
  9.4 232.4 %all-gather.14.cloned.1.call-start = ((), (), s32[]{:S(2)}) async-start(), calls=%async_computation.5 | async-start | bytes 2162688 | tf_op jit(solution)/shard_map/all_gather | solution.py:246
  10.0 310.6 %all-gather.18.cloned.1.call-start = ((), (), s32[]{:S(2)}) async-start(), calls=%async_computation.7 | async-start | bytes 8650752 | tf_op jit(solution)/shard_map/all_gather | solution.py:248
  10.6 388.8 %all-gather.16.cloned.1.call-start = ((), (), s32[]{:S(2)}) async-start(), calls=%async_computation.6 | async-start | bytes 8650752 | tf_op jit(solution)/shard_map/all_gather | solution.py:247
  11.1 467.2 %all-gather.20.cloned.1.call-start = ((), (), s32[]{:S(2)}) async-start(), calls=%async_computation.8 | async-start | bytes 8650752 | tf_op jit(solution)/shard_map/all_gather | solution.py:249
  11.9 1068.7 %reduce-scatter.3.cloned.1.call-start = ((), (), s32[]{:S(2)}) async-start(), calls=%async_computation.9 | async-start | bytes 51904512 | tf_op jit(solution)/shard_map/reduce_scatter | solution.py:281
  12.6 182.0 %copy-start.124 = (f32[64]{0:T(128)}, f32[64]{0:T(128)S(1)}, u32[]{:S(2)}) copy-start(f32[64]{0:T(128)S(1)} %convert_element_type.280) | copy-start | bytes 772
  13.3 181.0 %copy-start.122 = (f32[64]{0:T(128)}, f32[64]{0:T(128)S(1)}, u32[]{:S(2)}) copy-start(f32[64]{0:T(128)S(1)} %convert_element_type.285) | copy-start | bytes 772
  55.4 138.0 %copy-start.115 = (f32[128]{0:T(128)}, f32[128]{0:T(128)S(1)}, u32[]{:S(2)}) copy-start(f32[128]{0:T(128)S(1)} %fusion.105) | copy-start | bytes 1540
  55.9 142.4 %copy-start.118 = (f32[128]{0:T(128)}, f32[128]{0:T(128)S(1)}, u32[]{:S(2)}) copy-start(f32[128]{0:T(128)S(1)} %fusion.107) | copy-start | bytes 1540
  59.1 137.1 %copy-start.106 = (pred[128,128]{0,1:T(8,128)(4,1)}, pred[128,128]{0,1:T(8,128)(4,1)S(1)}, u32[]{:S(2)}) copy-start(pred[128,128]{0,1:T(8,128)(4,1)S(1)} %broadcast_compare_fusion.1) | copy-start | bytes 49156
  59.2 136.0 %copy-start.108 = (pred[128,128]{0,1:T(8,128)(4,1)}, pred[128,128]{0,1:T(8,128)(4,1)S(1)}, u32[]{:S(2)}) copy-start(pred[128,128]{0,1:T(8,128)(4,1)S(1)} %broadcast_compare_fusion) | copy-start | bytes 49156
  59.6 135.4 %copy-start.85 = (f32[128,32]{0,1:T(8,128)}, f32[128,32]{0,1:T(8,128)S(1)}, u32[]{:S(2)}) copy-start(f32[128,32]{0,1:T(8,128)S(1)} %get-tuple-element.112) | copy-start | bytes 49156
  59.6 135.4 %copy-start.87 = (f32[128,32]{0,1:T(8,128)}, f32[128,32]{0,1:T(8,128)S(1)}, u32[]{:S(2)}) copy-start(f32[128,32]{0,1:T(8,128)S(1)} %get-tuple-element.113) | copy-start | bytes 49156
  59.6 136.3 %copy-start.81 = (f32[128,32]{0,1:T(8,128)}, f32[128,32]{0,1:T(8,128)S(1)}, u32[]{:S(2)}) copy-start(f32[128,32]{0,1:T(8,128)S(1)} %get-tuple-element.88) | copy-start | bytes 49156
  59.6 136.3 %copy-start.83 = (f32[128,32]{0,1:T(8,128)}, f32[128,32]{0,1:T(8,128)S(1)}, u32[]{:S(2)}) copy-start(f32[128,32]{0,1:T(8,128)S(1)} %get-tuple-element.89) | copy-start | bytes 49156
  200.2 45.1 %copy-start.71 = (bf16[16,64,128]{2,1,0:T(8,128)(2,1)}, bf16[16,64,128]{2,1,0:T(8,128)(2,1)S(1)}, u32[]{:S(2)}) copy-start(bf16[16,64,128]{2,1,0:T(8,128)(2,1)S(1)} %convolution_convert_fusion.4) | copy-start | bytes 786436
  248.6 150.8 %copy-start.18 = (bf16[128,1024]{1,0:T(8,128)(2,1)}, bf16[128,1024]{1,0:T(8,128)(2,1)S(1)}, u32[]{:S(2)}) copy-start(bf16[128,1024]{1,0:T(8,128)(2,1)S(1)} %multiply_convert_fusion.7) | copy-start | bytes 786436
  478.3 10.1 copy-start
  488.4 10.9 slice-start
  491.4 7.9 slice-start.1
  539.6 11.8 copy-start.43
  545.4 28.3 %copy-start.47 = (bf16[128,16,64]{0,2,1:T(8,128)(2,1)}, bf16[128,16,64]{0,2,1:T(8,128)(2,1)S(1)}, u32[]{:S(2)}) copy-start(bf16[128,16,64]{0,2,1:T(8,128)(2,1)S(1)} %get-tuple-element.107) | copy-start | bytes 786436
  548.6 28.0 %copy-start.48 = (bf16[128,16,64]{0,2,1:T(8,128)(2,1)}, bf16[128,16,64]{0,2,1:T(8,128)(2,1)S(1)}, u32[]{:S(2)}) copy-start(bf16[128,16,64]{0,2,1:T(8,128)(2,1)S(1)} %get-tuple-element.103) | copy-start | bytes 786436
  557.3 8.2 copy-start.42
  565.5 8.2 copy-start.119
  584.9 8.3 copy-start.37
  651.1 616.2 %reduce-scatter.5.cloned.1.call-start = ((), (), s32[]{:S(2)}) async-start(), calls=%async_computation.10 | async-start | bytes 17301504 | tf_op jit(solution)/shard_map/reduce_scatter | solution.py:282
  677.4 42.0 %copy-start.17 = (f32[128,1024]{1,0:T(8,128)S(1)}, f32[128,1024]{1,0:T(8,128)}, u32[]{:S(2)}) copy-start(f32[128,1024]{1,0:T(8,128)} %copy-done.15) | copy-start | bytes 1572868
  677.4 42.0 %copy-start.21 = (bf16[128,4096]{1,0:T(8,128)(2,1)S(1)}, bf16[128,4096]{1,0:T(8,128)(2,1)}, u32[]{:S(2)}) copy-start(bf16[128,4096]{1,0:T(8,128)(2,1)} %get-tuple-element.49) | copy-start | bytes 3145732
  (119 other events, 267.9 us)
Sparse Core Ops, SparseCore 0:
  10.9 56.6 all-gather.7
  70.4 55.2 all-gather.11
  128.6 55.2 all-gather.9
  186.6 55.2 all-gather.13
  244.5 76.0 all-gather.17
  323.3 76.0 all-gather.15
  402.2 76.0 all-gather.19
  651.2 429.3 reduce-scatter.2
  1083.4 183.8 reduce-scatter.4
where the time goes:
time: 1280 us; the launch traced here: 1270 us
  waiting for transfers between devices  913 us (71%)
  matrix products  166 us (13%)
  blocking collectives  77.5 us (6%)
  other arithmetic  65.4 us (5%)
  local copies, waits for them, and re-layouts  35.8 us (3%)
  between operations  15.9 us (1%)
    reduce_scatter x1, waiting for transfers between devices, local(): lax.psum_scatter(rows_total, 'fsdp', scatter_dimension=0, tiled=True)  349 us
    reduce_scatter x1, waiting for transfers between devices, local(): lax.psum_scatter(down_total, 'fsdp', scatter_dimension=0, tiled=True)  183 us
    all_gather x1, waiting for transfers between devices, local(): lax.all_gather(w_down, 'fsdp', axis=0, tiled=True)  73 us
    all_gather x1, waiting for transfers between devices, local(): lax.all_gather(w_gate, 'fsdp', axis=0, tiled=True)  72.8 us
    all_gather x1, waiting for transfers between devices, local(): lax.all_gather(w_up, 'fsdp', axis=0, tiled=True)  72 us
    dot_general x14, matrix products, across(): lax.dot_general(left, right, (((0,), (0,)), ((), ())), preferred_element_...  70.6 us
    all_gather x1, waiting for transfers between devices, local(): lax.all_gather(w_key, 'fsdp', axis=0, tiled=True)  55.3 us
    all_gather x1, waiting for transfers between devices, local(): lax.all_gather(w_query, 'fsdp', axis=0, tiled=True)  54.2 us
  transfers between devices with their start and end apart: 9, of which 9 were waited for; matrix products, arithmetic and copies ran while one was open for 7% of the time, Pallas kernels for 0%

commit v1 on v0

--- a/solution.py
+++ b/solution.py
@@ -1,8 +1,11 @@
+import functools
 import math
 
 import jax
 import jax.numpy as jnp
 from jax import lax
+from jax.experimental import pallas as pl
+from jax.experimental.pallas import tpu as pltpu
 from jax.sharding import PartitionSpec as P
 
 EPSILON = 1e-05
@@ -194,7 +197,7 @@
     return (d_inputs + d_mixed, row_grads, grad_down, small)
 
 
-def local(
+def plain(
     tokens,
     segment_ids,
     variate_ids,
@@ -309,6 +312,753 @@
     )
 
 
+F32 = jnp.float32
+BF16 = jnp.bfloat16
+MESH = pl.DeviceIdType.MESH
+NT = (((1,), (1,)), ((), ()))
+TN = (((0,), (0,)), ((), ()))
+
+
+def mm(left, right, dims=(((1,), (0,)), ((), ()))):
+    return lax.dot_general(left, right, dims, preferred_element_type=F32)
+
+
+def at(start, size):
+    return pl.ds(pl.multiple_of(start, size), size)
+
+
+def lanes(start, size):
+    return pl.ds(pl.multiple_of(start, 128), size)
+
+
+def loop(count, body):
+    lax.fori_loop(0, count, lambda i, carry: (body(i), carry)[1], 0)
+
+
+def sizes_of(devices, tokens, w_query, w_gate, gain_query, bias):
+    seqs, length, width = tokens.shape
+    own_rows, hidden = w_query.shape[0], w_gate.shape[1]
+    return dict(
+        n=devices, S=seqs, L=length, D=width, FF=hidden, rows=own_rows, T=seqs * length,
+        G=devices // 4, Z=devices // 8, QC=width // 4, FC=hidden // 4, B=4 * own_rows,
+        HD=gain_query.shape[0], H=bias.shape[1],
+    )
+
+
+def fits(s):
+    return (
+        s["n"] % 8 == 0 and s["rows"] % 16 == 0 and s["L"] == 128 and s["HD"] == 64
+        and s["H"] * s["HD"] == s["D"] and s["QC"] % 128 == 0 and s["FF"] == 4 * s["D"]
+        and s["B"] % 128 == 0 and s["FC"] // 2 % s["B"] == 0 and s["FC"] == s["D"]
+    )
+
+
+def scratch_of(s):
+    n, S, L, D, rows, T, G, Z, QC, FC, B = (
+        s[k] for k in ("n", "S", "L", "D", "rows", "T", "G", "Z", "QC", "FC", "B")
+    )
+    Q = 4 * T
+    vm = pltpu.VMEM
+    return dict(
+        WA=vm((D, 4 * QC), BF16), WB=vm((D, 2 * FC), BF16), WC=vm((FC, D), BF16), WO=vm((D, D), BF16),
+        SA=vm((4, rows, 4 * QC), BF16), SB=vm((4, rows, 2 * FC), BF16),
+        h1Q=vm((Q, D), BF16), dyQ=vm((Q, D), BF16), attQ=vm((Q, D), BF16), h2Q=vm((Q, D), BF16),
+        qraw=vm((Q, QC), F32), kraw=vm((Q, QC), F32),
+        qr=vm((Q, QC), BF16), kr=vm((Q, QC), BF16), vb=vm((Q, QC), BF16),
+        PR=vm((4 * S, QC // 64, L, L), F32), CT=vm((Q, 128), F32), ST=vm((Q, 128), F32),
+        x1=vm((T, D), F32), dx1=vm((T, D), F32), acc=vm((T, D), F32),
+        hid=vm((Q, FC), BF16), dgdu=vm((Q, 2 * FC), BF16),
+        rsS=vm((3, T, D), BF16), rsR=vm((3, 3, T, D), BF16),
+        daS=vm((T, D), BF16), daR=vm((Q, QC), BF16), dattS=vm((T, D), BF16), dattR=vm((Q, QC), BF16),
+        YS=vm((2, Z, B, FC), BF16), YR=vm((4, Z, B, FC), BF16), ZR=vm((4, Z - 1, B, FC), BF16),
+        QS=vm((3, B, FC), BF16), QR=vm((3, 4, rows, FC), BF16),
+        idq=vm((4 * S, 8, L), F32),
+        GT=vm((3, 8, D), F32), GR=vm((4 + Z, 8, D), F32),
+        TT=vm((3, 8, D), F32), TR=vm((4 + Z, 8, D), F32),
+        HG=vm((4, QC // 128, 8, 128), F32), BG=vm((2, QC // 64, 8, 128), F32),
+        send=pltpu.SemaphoreType.DMA((192,)), recv=pltpu.SemaphoreType.DMA((192,)),
+    )
+
+
+INPUTS = (
+    "tok", "cot", "seg", "var", "tim", "wq", "wk", "wv", "wo", "wg", "wu", "wd", "gains", "hgain", "bias",
+)
+OUTPUTS = ("act", "ig", "gq", "gk", "gv", "go", "gg", "gu", "gd", "tot")
+
+
+def fused(s, names, *refs):
+    R = dict(zip(names, refs, strict=True))
+    n, S, L, D, rows, T, G, Z, QC, FC, B = (
+        s[k] for k in ("n", "S", "L", "D", "rows", "T", "G", "Z", "QC", "FC", "B")
+    )
+    HF = FC // 2
+    Q = 4 * T
+    me = lax.axis_index("fsdp")
+    r, c, xx, g = lax.rem(me, 4), lax.rem(me, 2), lax.rem(lax.div(me, 2), 2), lax.div(me, 4)
+    y, z = lax.rem(g, 2), lax.div(g, 2)
+    r_sib, r_par = r + 1 - 2 * c, r + 2 - 4 * xx
+    r_dia = r_sib + 2 - 4 * xx
+    sib, par, dia = me - r + r_sib, me - r + r_par, me - r + r_dia
+    peer = me + 4 - 8 * y
+    quad = ((sib, r_sib), (par, r_par), (dia, r_dia))
+
+    def at_z(step):
+        return lax.rem(z + step, Z)
+
+    def z_dev(step):
+        return at_z(step) * 8 + y * 4 + r
+
+    def z_src(step):
+        return lax.rem(z + Z - step, Z)
+
+    used = [0]
+    sent = []
+
+    def take(count=1):
+        used[0] += count
+        return used[0] - count
+
+    def remote(src, dst, device, sem=None):
+        sem = take() if sem is None else sem
+        return pltpu.make_async_remote_copy(
+            src_ref=src, dst_ref=dst, send_sem=R["send"].at[sem], recv_sem=R["recv"].at[sem],
+            device_id=(device,), device_id_type=MESH,
+        )
+
+    def go(copy):
+        copy.start()
+        sent.append(copy)
+        return copy
+
+    SA, SB, WA, WB, WC, WO = (R[k] for k in ("SA", "SB", "WA", "WB", "WC", "WO"))
+    for q in range(4):
+        for m, name in enumerate(("wq", "wk", "wv", "wo")):
+            SA[q, :, QC * m : QC * (m + 1)] = R[name][:, QC * q : QC * (q + 1)]
+        for j in range(G):
+            half, within = divmod(B * j, HF)
+            source = slice(B * (4 * j + q), B * (4 * j + q) + B)
+            SB[q, :, half * FC + within : half * FC + within + B] = R["wg"][:, source]
+            SB[q, :, half * FC + HF + within : half * FC + HF + within + B] = R["wu"][:, source]
+    own = at(B * g + rows * r, rows)
+    WA[own, :] = SA[r]
+    WB[own, :] = SB[r]
+    WC[at(B * g, B), :] = R["wd"][...]
+    idq = R["idq"]
+    for q in range(S):
+        idq[S * r + q, 0:1, :] = R["seg"][q : q + 1, :].astype(F32)
+        idq[S * r + q, 1:2, :] = R["var"][q : q + 1, :].astype(F32)
+        idq[S * r + q, 2:3, :] = R["tim"][q : q + 1, :].astype(F32)
+        idq[S * r + q, 3:8, :] = jnp.zeros((5, L), F32)
+    GT, GR = R["GT"], R["GR"]
+    GT[0] = R["gains"][...]
+    dyQ, h1Q, h2Q, attQ = R["dyQ"], R["h1Q"], R["h2Q"], R["attQ"]
+    dyQ[at(T * r, T), :] = R["cot"][...]
+
+    barrier = pltpu.get_barrier_semaphore()
+    others = [sib, par, dia, peer] + [z_dev(d) for d in range(1, Z)]
+    for device in others:
+        pl.semaphore_signal(barrier, inc=1, device_id=(device,), device_id_type=MESH)
+    pl.semaphore_wait(barrier, len(others))
+
+    def tile_sum(tile, got):
+        first = [remote(tile.at[0], got.at[i], dev) for i, (dev, _) in enumerate(quad)]
+        second = remote(tile.at[1], got.at[3], peer)
+        third = [remote(tile.at[2], got.at[4 + z], z_dev(d)) for d in range(1, Z)]
+
+        def round1():
+            for copy in first:
+                go(copy)
+
+        def round2():
+            for copy in first:
+                copy.wait_recv()
+            tile[1] = (tile[0] + got[0]) + (got[1] + got[2])
+            go(second)
+
+        def round3():
+            second.wait_recv()
+            value = tile[1] + got[3]
+            tile[2] = value
+            got[4 + z] = value
+            for copy in third:
+                go(copy)
+
+        def finish():
+            for copy in third:
+                copy.wait_recv()
+            value = got[4]
+            for i in range(1, Z):
+                value = value + got[4 + i]
+            return value
+
+        return round1, round2, round3, finish
+
+    def quad_gather(block):
+        to_sib, to_par = remote(block(r), block(r), sib), remote(block(r), block(r), par)
+        passed = remote(block(r_par), block(r_par), sib)
+
+        def start():
+            go(to_par)
+            go(to_sib)
+
+        def forward():
+            to_par.wait_recv()
+            go(passed)
+
+        def finish():
+            to_sib.wait_recv()
+            passed.wait_recv()
+
+        return start, forward, finish
+
+    chunks = [(WA, 0, 2 * QC), (WA, 2 * QC, 2 * QC)]
+    chunks += [(WB, HF * k, HF) for k in range(4)]
+    chunks += [(WC, 0, D // 2), (WC, D // 2, D // 2)]
+
+    def piece(k, group):
+        ref, start, size = chunks[k]
+        return ref.at[at(B * group, B), pl.ds(start, size)]
+
+    along = [[remote(piece(k, g), piece(k, g), z_dev(d)) for d in range(1, Z)] for k in range(8)]
+    over = [
+        [remote(piece(k, 2 * z_src(d) + y), piece(k, 2 * z_src(d) + y), peer) for d in range(Z)]
+        for k in range(8)
+    ]
+
+    def ag_start(k):
+        for copy in along[k]:
+            go(copy)
+        go(over[k][0])
+
+    def ag_forward(k):
+        for d in range(1, Z):
+            along[k][d - 1].wait_recv()
+            go(over[k][d])
+
+    def ag_finish(k):
+        for copy in over[k]:
+            copy.wait_recv()
+
+    g1, g2, g3, g_finish = tile_sum(GT, GR)
+    g1()
+    sendA = [remote(SA.at[q], WA.at[own], dev) for dev, q in quad]
+    sendB = [remote(SB.at[q], WB.at[own], dev) for dev, q in quad]
+    for copy in sendA:
+        go(copy)
+    mine = idq.at[pl.ds(S * r, S)]
+    sendI = [remote(mine, mine, dev) for dev, q in quad]
+    for copy in sendI:
+        go(copy)
+    for copy in sendB:
+        go(copy)
+    g2()
+    for copy in sendA:
+        copy.wait_recv()
+    ag_start(0)
+    ag_start(1)
+    g3()
+    for copy in sendB:
+        copy.wait_recv()
+    for k in range(2, 8):
+        ag_start(k)
+    for copy in sendI:
+        copy.wait_recv()
+
+    lane = lax.broadcasted_iota(jnp.int32, (L, 128), 1)
+    sub = lax.broadcasted_iota(jnp.int32, (L, 128), 0)
+    front = lax.rem(lane, 64) < 32
+    low = lane < 64
+    freq = jnp.exp(-math.log(10000.0) * lax.rem(lane, 32).astype(F32) / 32)
+    CT, ST = R["CT"], R["ST"]
+
+    def tables(q):
+        times = jnp.broadcast_to(idq[q, 2:3, :], (L, L)).T
+        angles = times * freq
+        CT[at(L * q, L), :] = jnp.cos(angles)
+        sine = jnp.sin(angles)
+        ST[at(L * q, L), :] = jnp.where(front, -sine, sine)
+
+    loop(4 * S, tables)
+
+    for copy in sent[:3]:
+        copy.wait_send()
+    del sent[:3]
+    GT[0] = g_finish()
+    tok = R["tok"]
+    step = 64
+
+    def norm_in(i):
+        x = tok[at(step * i, step), :].astype(F32)
+        inv = lax.rsqrt(jnp.mean(x * x, axis=-1, keepdims=True) + EPSILON)
+        h1Q[at(T * r + step * i, step), :] = (x * inv * GT[0, 0:1, :]).astype(BF16)
+
+    loop(T // step, norm_in)
+
+    def token_block(ref):
+        return lambda role: ref.at[at(T * role, T)]
+
+    h1_start, h1_forward, h1_finish = quad_gather(token_block(h1Q))
+    dy_start, dy_forward, dy_finish = quad_gather(token_block(dyQ))
+    att_start, att_forward, att_finish = quad_gather(lambda role: attQ.at[:, lanes(QC * role, QC)])
+    wo_start, wo_forward, wo_finish = quad_gather(lambda role: WO.at[:, lanes(QC * role, QC)])
+    h2_start, h2_forward, h2_finish = quad_gather(token_block(h2Q))
+    h1_start()
+    ag_forward(0)
+    h1_forward()
+    dy_start()
+    ag_forward(1)
+    h1_finish()
+    ag_finish(0)
+    ag_finish(1)
+
+    qraw, kraw, qr, kr, vb, PR = (R[k] for k in ("qraw", "kraw", "qr", "kr", "vb", "PR"))
+    hgain, bias = R["hgain"], R["bias"]
+
+    def swap(v):
+        return jnp.where(front, pltpu.roll(v, 96, 1), pltpu.roll(v, 32, 1))
+
+    def per_head(v):
+        first = jnp.sum(jnp.where(low, v, 0.0), axis=-1, keepdims=True)
+        second = jnp.sum(jnp.where(low, 0.0, v), axis=-1, keepdims=True)
+        return jnp.where(low, first, second)
+
+    def project_heads(q):
+        at_q = at(L * q, L)
+        value = mm(h1Q[at_q, :], WA[:, 0 : 3 * QC])
+        cosine, sine = CT[at_q, :], ST[at_q, :]
+        for m, (raw, ready) in enumerate(((qraw, qr), (kraw, kr))):
+            raw[at_q, :] = value[:, QC * m : QC * (m + 1)]
+            for j in range(QC // 128):
+                v = value[:, QC * m + 128 * j : QC * m + 128 * (j + 1)]
+                inv = lax.rsqrt(per_head(v * v) / 64 + EPSILON)
+                v = v * inv * hgain[m : m + 1, :]
+                v = v * cosine + swap(v) * sine
+                if m == 0:
+                    v = v * 0.125
+                ready[at_q, 128 * j : 128 * (j + 1)] = v.astype(BF16)
+        vb[at_q, :] = value[:, 2 * QC : 3 * QC].astype(BF16)
+
+    loop(4 * S, project_heads)
+    WO[:, lanes(QC * r, QC)] = WA[:, 3 * QC : 4 * QC]
+    wo_start()
+    ag_forward(2)
+    dy_forward()
+
+    def masks(q):
+        segment = jnp.broadcast_to(idq[q, 0:1, :], (L, L))
+        variate = jnp.broadcast_to(idq[q, 1:2, :], (L, L))
+        allowed = (segment == segment.T) & ((segment != 0.0) | (lane == sub))
+        return allowed, variate == variate.T
+
+    heads = [jnp.where(low, 1.0, 0.0).astype(BF16), jnp.where(low, 0.0, 1.0).astype(BF16)]
+
+    def attend(q):
+        at_q = at(L * q, L)
+        allowed, same = masks(q)
+        for j in range(QC // 128):
+            tile = slice(128 * j, 128 * (j + 1))
+            q2, k2, v2 = qr[at_q, tile], kr[at_q, tile], vb[at_q, tile]
+            outs = []
+            for h in range(2):
+                head = 2 * j + h
+                index = QC // 64 * r + head
+                score = mm(q2 * heads[h], k2, NT) + jnp.where(same, bias[1, index], bias[0, index])
+                score = jnp.where(allowed, score, -1000000000.0)
+                e = jnp.exp(score - jnp.max(score, axis=-1, keepdims=True))
+                p = e / jnp.sum(e, axis=-1, keepdims=True)
+                PR[q, head] = p
+                outs.append(mm(p.astype(BF16), v2))
+            attQ[at_q, lanes(QC * r + 128 * j, 128)] = jnp.where(low, outs[0], outs[1]).astype(BF16)
+
+    loop(4 * S, attend)
+    att_start()
+    wo_forward()
+    ag_forward(3)
+    att_forward()
+    wo_finish()
+    att_finish()
+
+    x1, dx1, acc = R["x1"], R["dx1"], R["acc"]
+
+    def mix(i):
+        x = tok[at(step * i, step), :].astype(F32) + mm(attQ[at(T * r + step * i, step), :], WO[...])
+        x1[at(step * i, step), :] = x
+        inv = lax.rsqrt(jnp.mean(x * x, axis=-1, keepdims=True) + EPSILON)
+        h2Q[at(T * r + step * i, step), :] = (x * inv * GT[0, 1:2, :]).astype(BF16)
+
+    loop(T // step, mix)
+    h2_start()
+    ag_forward(4)
+    h2_forward()
+    dy_finish()
+    ag_forward(5)
+    h2_finish()
+    for k in range(2, 6):
+        ag_finish(k)
+
+    hid, dgdu = R["hid"], R["dgdu"]
+
+    def hidden(i):
+        at_i = at(L * i, L)
+        for half in range(2):
+            both = mm(h2Q[at_i, :], WB[:, half * FC : (half + 1) * FC])
+            gate, up = both[:, 0:HF], both[:, HF:FC]
+            hid[at_i, half * HF : (half + 1) * HF] = (gate / (1.0 + jnp.exp(-gate)) * up).astype(BF16)
+
+    loop(4 * S, hidden)
+    ag_forward(6)
+
+    YS, YR, ZR, QS, QR = (R[k] for k in ("YS", "YR", "ZR", "QS", "QR"))
+    y_sem, z_sem = [take(Z) for _ in range(4)], [take(Z - 1) for _ in range(4)]
+
+    def gradient(unit, group, store):
+        at_g = lanes(B * group, B)
+        if unit == 0:
+            store(slice(0, FC), mm(hid[:, at_g], dyQ[...], TN))
+        elif unit < 3:
+            store(slice(0, FC), mm(h2Q[:, at_g], dgdu[:, (unit - 1) * FC : unit * FC], TN))
+        else:
+            store(slice(0, 3 * QC), mm(h1Q[:, at_g], hid[:, 0 : 3 * QC], TN))
+            store(slice(3 * QC, 4 * QC), mm(attQ[:, at_g], R["daR"][...], TN))
+
+    def y_copy(unit, i):
+        return remote(YS.at[unit % 2, i], YR.at[unit, i], peer, y_sem[unit] + i)
+
+    def z_copy(unit, i):
+        return remote(YR.at[unit, i], ZR.at[unit, i - 1], z_dev(i), z_sem[unit] + i - 1)
+
+    def order(i):
+        return lax.rem(i + 1, Z)
+
+    def rs_first(unit):
+        if unit >= 2:
+            for i in range(Z):
+                y_copy(unit - 2, i).wait_send()
+
+        def body(i):
+            d = order(i)
+
+            def store(cols, value):
+                YS[unit % 2, d, :, cols] = value.astype(BF16)
+
+            gradient(unit, 2 * at_z(d) + 1 - y, store)
+            y_copy(unit, d).start()
+
+        loop(Z, body)
+
+    def rs_second(unit):
+        def body(i):
+            d = order(i)
+            y_copy(unit, d).wait_recv()
+
+            def store(cols, value):
+                YR[unit, d, :, cols] = (value + YR[unit, d, :, cols].astype(F32)).astype(BF16)
+
+            gradient(unit, 2 * at_z(d) + y, store)
+
+            @pl.when(d != 0)
+            def _():
+                z_copy(unit, d).start()
+
+        loop(Z, body)
+
+    quad_copies = {}
+
+    def rs_third(unit):
+        for i in range(1, Z):
+            z_copy(unit, i).wait_recv()
+        width = 256
+        for j in range(FC // width):
+            cols = slice(width * j, width * (j + 1))
+            value = YR[unit, 0, :, cols].astype(F32)
+            for i in range(1, Z):
+                value = value + ZR[unit, i - 1, :, cols].astype(F32)
+            if unit == 0:
+                R["gd"][:, cols] = value
+            else:
+                QS[unit - 1, :, cols] = value.astype(BF16)
+        if unit:
+            QR[unit - 1, r] = QS[unit - 1, at(rows * r, rows), :]
+            quad_copies[unit] = [
+                go(remote(QS.at[unit - 1, at(rows * q, rows)], QR.at[unit - 1, r], dev)) for dev, q in quad
+            ]
+
+    def rs_last(unit):
+        for copy in quad_copies[unit]:
+            copy.wait_recv()
+        for q in range(4):
+            if unit == 3:
+                for m, name in enumerate(("gq", "gk", "gv", "go")):
+                    R[name][:, QC * q : QC * (q + 1)] = QR[unit - 1, q, :, QC * m : QC * (m + 1)].astype(F32)
+            else:
+                for j in range(G):
+                    half, within = divmod(B * j, HF)
+                    if half == unit - 1:
+                        target = slice(B * (4 * j + q), B * (4 * j + q) + B)
+                        R["gg"][:, target] = QR[unit - 1, q, :, within : within + B].astype(F32)
+                        R["gu"][:, target] = QR[unit - 1, q, :, HF + within : HF + within + B].astype(F32)
+
+    rsS, rsR = R["rsS"], R["rsR"]
+
+    def quad_sum(kind, prepare_block, partial):
+        width = 512
+        tiles = [slice(width * j, width * (j + 1)) for j in range(D // width)]
+        copies = [
+            remote(rsS.at[0], rsR.at[kind, 0], sib),
+            remote(rsS.at[1], rsR.at[kind, 1], sib),
+            remote(rsS.at[2], rsR.at[kind, 2], par),
+        ]
+
+        def blocks(role, store):
+            def body(i):
+                for cols in tiles:
+                    store(at(L * i, L), cols, partial(at(T * role + L * i, L), cols))
+
+            loop(T // L, body)
+
+        def to_dia(at_i, cols, value):
+            rsS[1, at_i, cols] = value.astype(BF16)
+
+        def to_par(at_i, cols, value):
+            rsS[2, at_i, cols] = (value + rsR[kind, 1, at_i, cols].astype(F32)).astype(BF16)
+
+        def to_sib(at_i, cols, value):
+            rsS[0, at_i, cols] = value.astype(BF16)
+
+        def keep(at_i, cols, value):
+            acc[at_i, cols] = value
+
+        prepare_block(r_dia)
+        blocks(r_dia, to_dia)
+        copies[1].start()
+        prepare_block(r_par)
+        copies[1].wait_recv()
+        blocks(r_par, to_par)
+        copies[2].start()
+        prepare_block(r_sib)
+        blocks(r_sib, to_sib)
+        copies[0].start()
+        prepare_block(r)
+        blocks(r, keep)
+
+        def finish():
+            copies[0].wait_recv()
+            copies[2].wait_recv()
+            for copy in copies:
+                copy.wait_send()
+
+        return finish
+
+    def summed(kind, at_i):
+        return acc[at_i, :] + (rsR[kind, 0, at_i, :].astype(F32) + rsR[kind, 2, at_i, :].astype(F32))
+
+    rs_first(0)
+    ag_forward(7)
+    rs_second(0)
+    ag_finish(6)
+    ag_finish(7)
+
+    def ffn_back(role):
+        def body(i):
+            at_i = at(T * role + L * i, L)
+            for half in range(2):
+                both = mm(h2Q[at_i, :], WB[:, half * FC : (half + 1) * FC])
+                gate, up = both[:, 0:HF], both[:, HF:FC]
+                d_hidden = mm(dyQ[at_i, :], WC[half * HF : (half + 1) * HF, :], NT)
+                sigma = 1.0 / (1.0 + jnp.exp(-gate))
+                d_up = d_hidden * (gate * sigma)
+                d_gate = d_hidden * up * (sigma * (1.0 + gate * (1.0 - sigma)))
+                dgdu[at_i, half * FC : half * FC + HF] = d_gate.astype(BF16)
+                dgdu[at_i, half * FC + HF : (half + 1) * FC] = d_up.astype(BF16)
+
+        loop(T // L, body)
+
+    def nothing(role):
+        return None
+
+    h2_sum = quad_sum(0, ffn_back, lambda at_i, cols: mm(dgdu[at_i, :], WB[cols, :], NT))
+    rs_first(1)
+    h2_sum()
+
+    TT, TR = R["TT"], R["TR"]
+    daS, daR, dattS, dattR = (R[k] for k in ("daS", "daR", "dattS", "dattR"))
+    TT[0] = jnp.zeros((8, D), F32)
+
+    def norm_back(v, d_out, gain, row):
+        inv = lax.rsqrt(jnp.mean(v * v, axis=-1, keepdims=True) + EPSILON)
+        TT[0, row : row + 1, :] += jnp.sum(d_out * (v * inv), axis=0, keepdims=True)
+        d = d_out * gain
+        return inv * d - v * (inv * inv * inv * jnp.mean(d * v, axis=-1, keepdims=True))
+
+    def mix_back(i):
+        at_i = at(step * i, step)
+        d = norm_back(x1[at_i, :], summed(0, at_i), GT[0, 1:2, :], 1)
+        d = d + R["cot"][at_i, :].astype(F32)
+        dx1[at_i, :] = d
+        daS[at_i, :] = d.astype(BF16)
+
+    loop(T // step, mix_back)
+    sendD = [remote(daS.at[:, lanes(QC * q, QC)], daR.at[at(T * r, T)], dev) for dev, q in quad]
+    sendT = [remote(dattS.at[:, lanes(QC * q, QC)], dattR.at[at(T * r, T)], dev) for dev, q in quad]
+
+    def out_back(i):
+        at_i = at(step * i, step)
+        dattS[at_i, :] = mm(daS[at_i, :], WO[...], NT).astype(BF16)
+
+    loop(T // step, out_back)
+    for copy in sendT:
+        go(copy)
+    for copy in sendD:
+        go(copy)
+    dattR[at(T * r, T), :] = dattS[:, lanes(QC * r, QC)]
+    daR[at(T * r, T), :] = daS[:, lanes(QC * r, QC)]
+    rs_second(1)
+    rs_first(2)
+
+    out_sum = quad_sum(1, nothing, lambda at_i, cols: mm(hid[at_i, :], WC[:, cols]))
+    out_sum()
+
+    def write_out(i):
+        at_i = at(step * i, step)
+        R["act"][at_i, :] = (x1[at_i, :] + summed(1, at_i)).astype(BF16)
+
+    loop(T // step, write_out)
+    for copy in sendT:
+        copy.wait_recv()
+
+    HG, BG = R["HG"], R["BG"]
+    HG[...] = jnp.zeros(HG.shape, F32)
+    BG[...] = jnp.zeros(BG.shape, F32)
+
+    def fold(v):
+        return jnp.sum(v.reshape(L // 8, 8, 128), axis=0)
+
+    def prepare_back(raw, d, m, j, cosine, sine, factor):
+        if factor != 1.0:
+            d = d * factor
+        d = d * cosine - swap(d) * sine
+        inv = lax.rsqrt(per_head(raw * raw) / 64 + EPSILON)
+        HG[m, j] += fold(d * (raw * inv))
+        d = d * hgain[m : m + 1, :]
+        return inv * d - raw * (inv * inv * inv * (per_head(d * raw) / 64))
+
+    def attend_back(q):
+        at_q = at(L * q, L)
+        _, same = masks(q)
+        cosine, sine = CT[at_q, :], ST[at_q, :]
+        for j in range(QC // 128):
+            tile = slice(128 * j, 128 * (j + 1))
+            q2, k2, v2, d2 = qr[at_q, tile], kr[at_q, tile], vb[at_q, tile], dattR[at_q, tile]
+            dq, dk, dv = [], [], []
+            for h in range(2):
+                p = PR[q, 2 * j + h]
+                dp = mm(d2 * heads[h], v2, NT)
+                ds = (p * (dp - jnp.sum(p * dp, axis=-1, keepdims=True))).astype(BF16)
+                wide = ds.astype(F32)
+                BG[0, 2 * j + h] += fold(jnp.where(same, 0.0, wide))
+                BG[1, 2 * j + h] += fold(jnp.where(same, wide, 0.0))
+                dv.append(mm(p.astype(BF16), d2, TN))
+                dq.append(mm(ds, k2))
+                dk.append(mm(ds, q2, TN))
+            d_query = jnp.where(low, dq[0], dq[1])
+            d_key = jnp.where(low, dk[0], dk[1])
+            d_query = prepare_back(qraw[at_q, tile], d_query, 0, j, cosine, sine, 0.125)
+            d_key = prepare_back(kraw[at_q, tile], d_key, 1, j, cosine, sine, 1.0)
+            hid[at_q, tile] = d_query.astype(BF16)
+            hid[at_q, QC + 128 * j : QC + 128 * (j + 1)] = d_key.astype(BF16)
+            hid[at_q, 2 * QC + 128 * j : 2 * QC + 128 * (j + 1)] = jnp.where(low, dv[0], dv[1]).astype(BF16)
+
+    loop(4 * S, attend_back)
+    rs_second(2)
+    for copy in sendD:
+        copy.wait_recv()
+    rs_first(3)
+    rs_third(0)
+    in_sum = quad_sum(2, nothing, lambda at_i, cols: mm(hid[at_i, 0 : 3 * QC], WA[cols, 0 : 3 * QC], NT))
+    rs_third(1)
+    rs_second(3)
+    in_sum()
+
+    def input_back(i):
+        at_i = at(step * i, step)
+        d = norm_back(tok[at_i, :].astype(F32), summed(2, at_i), GT[0, 0:1, :], 0)
+        R["ig"][at_i, :] = (dx1[at_i, :] + d).astype(BF16)
+
+    loop(T // step, input_back)
+
+    for m in range(2):
+        value = HG[m, 0]
+        for j in range(1, QC // 128):
+            value = value + HG[m, j]
+        TT[0, 2:3, 128 * m : 128 * (m + 1)] = jnp.sum(value, axis=0, keepdims=True)
+    spot = lax.broadcasted_iota(jnp.int32, (1, 128), 1)
+    for m in range(2):
+        line = jnp.zeros((1, 128), F32)
+        for h in range(QC // 64):
+            line = line + jnp.where(spot == QC // 64 * r + h, jnp.sum(BG[m, h]), 0.0)
+        TT[0, 3 + m : 4 + m, 0:128] = line
+    t1, t2, t3, t_finish = tile_sum(TT, TR)
+    t1()
+    rs_third(2)
+    t2()
+    rs_last(1)
+    t3()
+    rs_last(2)
+    R["tot"][...] = t_finish()
+    rs_third(3)
+    rs_last(3)
+    for copy in sent:
+        copy.wait_send()
+    for unit in range(4):
+        for i in range(Z):
+            if unit >= 2:
+                y_copy(unit, i).wait_send()
+            if i:
+                z_copy(unit, i).wait_send()
+
+
+def layer(s, tokens, segment_ids, variate_ids, time_ids, w_query, w_key, w_value, w_out, w_gate, w_up, w_down,
+          gain_attn, gain_ffn, gain_query, gain_key, variate_bias, cotangent):
+    D, T, rows, B, FF = s["D"], s["T"], s["rows"], s["B"], s["FF"]
+    owner = lax.axis_index("fsdp")
+    pair = jnp.stack([gain_attn, gain_ffn]).astype(F32)
+    gains = lax.dynamic_update_slice(jnp.zeros((8, D), F32), pair, (0, owner * rows))
+    hgain = jnp.tile(jnp.stack([gain_query, gain_key]).astype(F32), (4, 2))
+    scratch = scratch_of(s)
+    names = INPUTS + OUTPUTS + tuple(scratch)
+    vmem = pl.BlockSpec(memory_space=pltpu.VMEM)
+    small = [(rows, D)] * 4 + [(rows, FF)] * 2 + [(B, D), (8, D)]
+    outs = pl.pallas_call(
+        functools.partial(fused, s, names),
+        out_shape=[jax.ShapeDtypeStruct((T, D), BF16)] * 2 + [jax.ShapeDtypeStruct(d, F32) for d in small],
+        in_specs=[vmem] * (len(INPUTS) - 1) + [pl.BlockSpec(memory_space=pltpu.SMEM)],
+        out_specs=[vmem] * len(OUTPUTS),
+        scratch_shapes=list(scratch.values()),
+        compiler_params=pltpu.CompilerParams(
+            collective_id=0, has_side_effects=True, vmem_limit_bytes=64 << 20
+        ),
+        name="fused_layer",
+    )(
+        tokens.reshape(T, D), cotangent.reshape(T, D), segment_ids, variate_ids, time_ids,
+        w_query, w_key, w_value, w_out, w_gate, w_up, w_down, gains, hgain, variate_bias.astype(F32),
+    )
+    act, ig, gq, gk, gv, go, gg, gu, gd, tot = outs
+    attn_own = lax.dynamic_slice(tot, (0, owner * rows), (1, rows)).reshape(rows)
+    ffn_own = lax.dynamic_slice(tot, (1, owner * rows), (1, rows)).reshape(rows)
+    HD, H = s["HD"], s["H"]
+    return (
+        act.reshape(tokens.shape), ig.reshape(tokens.shape), gq, gk, gv, go, gg, gu, gd, attn_own, ffn_own,
+        tot[2, 0:HD] + tot[2, HD : 2 * HD], tot[2, 128 : 128 + HD] + tot[2, 128 + HD : 128 + 2 * HD],
+        tot[3:5, 0:H],
+    )
+
+
+def local(tokens, segment_ids, variate_ids, time_ids, *rest):
+    s = sizes_of(lax.axis_size("fsdp"), tokens, rest[0], rest[4], rest[9], rest[11])
+    chosen = functools.partial(layer, s) if fits(s) else plain
+    return chosen(tokens, segment_ids, variate_ids, time_ids, *rest)
+
+
 def solution(mesh):
     placed = (
         P("fsdp", None, None),

time: 1280 us -> 336 us (0.26)
  waiting for transfers between devices: 913 us -> 0 us
  Pallas kernels: 0 us -> 316 us
  matrix products: 166 us -> 0 us
  blocking collectives: 77.5 us -> 0 us
  other arithmetic: 65.4 us -> 1.93 us
  local copies, waits for them, and re-layouts: 35.8 us -> 15.9 us
  between operations: 15.9 us -> 0.73 us
    reduce_scatter x2 -> x0, waiting for transfers between devices: 532 us -> none  [the longest x1 349 us: local(): lax.psum_scatter(rows_total, 'fsdp', scatter_dimension=0, tiled=True)]
    all_gather x7 -> x0, waiting for transfers between devices: 377 us -> none  [the longest x1 73 us: local(): lax.all_gather(w_down, 'fsdp', axis=0, tiled=True)]
    pallas_call x0 -> x1, Pallas kernels: none -> 316 us  [layer(): pl.pallas_call(functools.partial(fused, s, names), out_shape=[jax.ShapeDt...]
    dot_general x54 -> x0, matrix products: 166 us -> none  [the longest x14 70.6 us: across(): lax.dot_general(left, right, (((0,), (0,)), ((), ())), preferred_element_...]
    add x9 -> x1, other arithmetic: 51.3 us -> 1.35 us  [layer(): tot[2, 128:128 + HD] + tot[2, 128 + HD:128 + 2 * HD]]
    psum x1 -> x0, blocking collectives: 39 us -> none  [local(): lax.psum((side_totals[0], side_totals[1], side_totals[2], side_totals[3],...]
    unnamed x1 -> x0, blocking collectives: 38.5 us -> none
  transfers between devices with their start and end apart: 9 -> 0, of which waited for: 9 -> 0; matrix products, arithmetic and copies ran while one was open for 7% -> 0% of each run, Pallas kernels for 0% -> 0%
where the time goes in v1:
time: 336 us; the launch traced here: 335 us
  Pallas kernels  316 us (94%)
  local copies, waits for them, and re-layouts  15.9 us (5%)
    pallas_call x1, Pallas kernels, layer(): pl.pallas_call(functools.partial(fused, s, names), out_shape=[jax.ShapeDt...  316 us
    unnamed x35, local copies, waits for them, and re-layouts  10.4 us

profile of v1, /device:TPU:25, one launch (start us, length us, event | category | flops | bytes accessed | tf_op | source)
XLA Modules:
  0.0 334.5 jit_solution(668715769910647169)
XLA Ops:
  0.6 0.0 copy-start.8
  0.7 0.0 copy-start.9
  0.7 0.6 copy-done.8
  1.3 0.0 copy-done.9
  1.3 0.6 broadcast_in_dim.3
  1.9 1.6 dynamic_update_slice.3.refs_12_
  3.6 0.0 copy-start.10
  3.6 0.0 copy-start.11
  3.6 0.6 copy-done.10
  4.2 0.0 copy-done.11
  4.2 0.0 copy-start.12
  4.3 0.7 tile.10.refs_13_
  4.9 0.6 convert_element_type.15.refs_14_
  5.5 316.0 %fused_layer.1 = (bf16[256,1024]{1,0:T(8,128)(2,1)}, bf16[256,1024]{1,0:T(8,128)(2,1)}, f32[32,1024]{1,0:T(8,128)}, f32[32,1024]{1,0:T(8,128)}, f32[32,1024]{1,0...) custom-call(bf16[256,1024]{1,0:T(8,128)(2,1)} %bitcast.18, ...), custom_call_target="tpu_custom_call" | custom-call | tf_op jit(solution)/shard_map/fused_layer/pallas_call | solution.py:1031
  321.5 1.4 dynamic-slice_bitcast_fusion
  322.8 1.3 add_bitcast_fusion
  324.2 1.2 slice.19
  325.4 1.9 copy.41
  327.4 0.0 copy-done.3
  327.4 0.8 copy.42
  328.2 0.2 copy-done.7
  328.4 0.7 copy.43
  329.0 0.0 copy-done.6
  329.0 0.7 copy.44
  329.7 0.7 copy.45
  330.3 0.3 copy-done.4
  330.6 0.7 copy.46
  331.3 0.8 copy.47
  332.1 0.4 copy-done.1
  332.5 0.8 copy.48
  333.3 0.4 copy-done
  333.8 0.8 copy.49
  (14 shorter events, 0.0 us)
Async XLA Ops:
  0.6 0.7 copy-start.8
  0.7 0.7 copy-start.9
  3.6 0.7 copy-start.10
  3.6 0.7 copy-start.11
  4.2 0.7 copy-start.12
  325.4 1.9 copy-start.3
  327.4 1.0 copy-start.7
  327.4 1.7 copy-start.6
  327.4 2.3 copy-start.5
  328.4 2.9 copy-start.2
  329.7 1.0 copy-start.4
  331.3 1.2 copy-start.1
  332.5 1.2 copy-start

commit v2 on v1

--- a/solution.py
+++ b/solution.py
@@ -370,7 +370,7 @@
         hid=vm((Q, FC), BF16), dgdu=vm((Q, 2 * FC), BF16),
         rsS=vm((3, T, D), BF16), rsR=vm((3, 3, T, D), BF16),
         daS=vm((T, D), BF16), daR=vm((Q, QC), BF16), dattS=vm((T, D), BF16), dattR=vm((Q, QC), BF16),
-        YS=vm((2, Z, B, FC), BF16), YR=vm((4, Z, B, FC), BF16), ZR=vm((4, Z - 1, B, FC), BF16),
+        YS=vm((3, Z, B, FC), BF16), YR=vm((4, Z, B, FC), BF16), ZR=vm((4, Z - 1, B, FC), BF16),
         QS=vm((3, B, FC), BF16), QR=vm((3, 4, rows, FC), BF16),
         idq=vm((4 * S, 8, L), F32),
         GT=vm((3, 8, D), F32), GR=vm((4 + Z, 8, D), F32),
@@ -381,9 +381,9 @@
 
 
 INPUTS = (
-    "tok", "cot", "seg", "var", "tim", "wq", "wk", "wv", "wo", "wg", "wu", "wd", "gains", "hgain", "bias",
+    "tok", "cot", "seg", "var", "tim", "wq", "wk", "wv", "wo", "wg", "wu", "wd", "small",
 )
-OUTPUTS = ("act", "ig", "gq", "gk", "gv", "go", "gg", "gu", "gd", "tot")
+OUTPUTS = ("act", "ig", "gd", "parts", "tot")
 
 
 def fused(s, names, *refs):
@@ -450,7 +450,9 @@
         idq[S * r + q, 2:3, :] = R["tim"][q : q + 1, :].astype(F32)
         idq[S * r + q, 3:8, :] = jnp.zeros((5, L), F32)
     GT, GR = R["GT"], R["GR"]
-    GT[0] = R["gains"][...]
+    small = R["small"]
+    GT[0] = jnp.zeros((8, D), F32)
+    GT[0, :, lanes(128 * lax.div(rows * me, 128), 128)] = pltpu.roll(small[...], lax.rem(rows * me, 128), 1)
     dyQ, h1Q, h2Q, attQ = R["dyQ"], R["h1Q"], R["h2Q"], R["attQ"]
     dyQ[at(T * r, T), :] = R["cot"][...]
 
@@ -462,8 +464,8 @@
 
     def tile_sum(tile, got):
         first = [remote(tile.at[0], got.at[i], dev) for i, (dev, _) in enumerate(quad)]
-        second = remote(tile.at[1], got.at[3], peer)
-        third = [remote(tile.at[2], got.at[4 + z], z_dev(d)) for d in range(1, Z)]
+        second = [remote(tile.at[1], got.at[4 + z], z_dev(d)) for d in range(1, Z)]
+        third = remote(tile.at[2], got.at[3], peer)
 
         def round1():
             for copy in first:
@@ -472,24 +474,24 @@
         def round2():
             for copy in first:
                 copy.wait_recv()
-            tile[1] = (tile[0] + got[0]) + (got[1] + got[2])
-            go(second)
+            value = (tile[0] + got[0]) + (got[1] + got[2])
+            tile[1] = value
+            got[4 + z] = value
+            for copy in second:
+                go(copy)
 
         def round3():
-            second.wait_recv()
-            value = tile[1] + got[3]
-            tile[2] = value
-            got[4 + z] = value
-            for copy in third:
-                go(copy)
-
-        def finish():
-            for copy in third:
+            for copy in second:
                 copy.wait_recv()
             value = got[4]
             for i in range(1, Z):
                 value = value + got[4 + i]
-            return value
+            tile[2] = value
+            go(third)
+
+        def finish():
+            third.wait_recv()
+            return tile[2] + got[3]
 
         return round1, round2, round3, finish
 
@@ -511,9 +513,8 @@
 
         return start, forward, finish
 
-    chunks = [(WA, 0, 2 * QC), (WA, 2 * QC, 2 * QC)]
+    chunks = [(WA, 0, 2 * QC), (WA, 2 * QC, 2 * QC), (WC, 0, D // 2), (WC, D // 2, D // 2)]
     chunks += [(WB, HF * k, HF) for k in range(4)]
-    chunks += [(WC, 0, D // 2), (WC, D // 2, D // 2)]
 
     def piece(k, group):
         ref, start, size = chunks[k]
@@ -528,12 +529,16 @@
     def ag_start(k):
         for copy in along[k]:
             go(copy)
+
+    def ag_own(k):
         go(over[k][0])
 
     def ag_forward(k):
         for d in range(1, Z):
             along[k][d - 1].wait_recv()
             go(over[k][d])
+        if k + 2 < len(chunks):
+            ag_own(k + 2)
 
     def ag_finish(k):
         for copy in over[k]:
@@ -549,18 +554,13 @@
     sendI = [remote(mine, mine, dev) for dev, q in quad]
     for copy in sendI:
         go(copy)
-    for copy in sendB:
-        go(copy)
     g2()
     for copy in sendA:
         copy.wait_recv()
-    ag_start(0)
-    ag_start(1)
-    g3()
-    for copy in sendB:
-        copy.wait_recv()
-    for k in range(2, 8):
+    for k in range(4):
         ag_start(k)
+        if k < 2:
+            ag_own(k)
     for copy in sendI:
         copy.wait_recv()
 
@@ -578,8 +578,9 @@
         sine = jnp.sin(angles)
         ST[at(L * q, L), :] = jnp.where(front, -sine, sine)
 
-    loop(4 * S, tables)
-
+    loop(2 * S, tables)
+    g3()
+    loop(2 * S, lambda q: tables(2 * S + q))
     for copy in sent[:3]:
         copy.wait_send()
     del sent[:3]
@@ -603,16 +604,26 @@
     wo_start, wo_forward, wo_finish = quad_gather(lambda role: WO.at[:, lanes(QC * role, QC)])
     h2_start, h2_forward, h2_finish = quad_gather(token_block(h2Q))
     h1_start()
+    for copy in sendB:
+        go(copy)
     ag_forward(0)
     h1_forward()
+    ag_forward(1)
+    for copy in sendB:
+        copy.wait_recv()
+    for k in range(4, 8):
+        ag_start(k)
     dy_start()
-    ag_forward(1)
     h1_finish()
     ag_finish(0)
     ag_finish(1)
 
     qraw, kraw, qr, kr, vb, PR = (R[k] for k in ("qraw", "kraw", "qr", "kr", "vb", "PR"))
-    hgain, bias = R["hgain"], R["bias"]
+    spot = lax.broadcasted_iota(jnp.int32, (1, 128), 1)
+    bias = [
+        [jnp.sum(jnp.where(spot == QC // 64 * r + h, small[4 + m : 5 + m, :], 0.0)) for h in range(QC // 64)]
+        for m in range(2)
+    ]
 
     def swap(v):
         return jnp.where(front, pltpu.roll(v, 96, 1), pltpu.roll(v, 32, 1))
@@ -631,7 +642,7 @@
             for j in range(QC // 128):
                 v = value[:, QC * m + 128 * j : QC * m + 128 * (j + 1)]
                 inv = lax.rsqrt(per_head(v * v) / 64 + EPSILON)
-                v = v * inv * hgain[m : m + 1, :]
+                v = v * inv * small[2 + m : 3 + m, :]
                 v = v * cosine + swap(v) * sine
                 if m == 0:
                     v = v * 0.125
@@ -641,8 +652,8 @@
     loop(4 * S, project_heads)
     WO[:, lanes(QC * r, QC)] = WA[:, 3 * QC : 4 * QC]
     wo_start()
+    dy_forward()
     ag_forward(2)
-    dy_forward()
 
     def masks(q):
         segment = jnp.broadcast_to(idq[q, 0:1, :], (L, L))
@@ -661,8 +672,7 @@
             outs = []
             for h in range(2):
                 head = 2 * j + h
-                index = QC // 64 * r + head
-                score = mm(q2 * heads[h], k2, NT) + jnp.where(same, bias[1, index], bias[0, index])
+                score = mm(q2 * heads[h], k2, NT) + jnp.where(same, bias[1][head], bias[0][head])
                 score = jnp.where(allowed, score, -1000000000.0)
                 e = jnp.exp(score - jnp.max(score, axis=-1, keepdims=True))
                 p = e / jnp.sum(e, axis=-1, keepdims=True)
@@ -672,10 +682,12 @@
 
     loop(4 * S, attend)
     att_start()
+    ag_forward(3)
     wo_forward()
-    ag_forward(3)
+    ag_forward(4)
     att_forward()
     wo_finish()
+    dy_finish()
     att_finish()
 
     x1, dx1, acc = R["x1"], R["dx1"], R["acc"]
@@ -688,25 +700,36 @@
 
     loop(T // step, mix)
     h2_start()
-    ag_forward(4)
+    ag_forward(5)
+    ag_finish(2)
+    ag_finish(3)
     h2_forward()
-    dy_finish()
-    ag_forward(5)
-    h2_finish()
-    for k in range(2, 6):
-        ag_finish(k)
+    ag_finish(4)
+    ag_finish(5)
 
     hid, dgdu = R["hid"], R["dgdu"]
 
-    def hidden(i):
-        at_i = at(L * i, L)
-        for half in range(2):
+    def ffn(half, role):
+        def body(i):
+            at_i = at(T * role + L * i, L)
             both = mm(h2Q[at_i, :], WB[:, half * FC : (half + 1) * FC])
             gate, up = both[:, 0:HF], both[:, HF:FC]
-            hid[at_i, half * HF : (half + 1) * HF] = (gate / (1.0 + jnp.exp(-gate)) * up).astype(BF16)
-
-    loop(4 * S, hidden)
+            sigma = 1.0 / (1.0 + jnp.exp(-gate))
+            silu = gate * sigma
+            hid[at_i, half * HF : (half + 1) * HF] = (silu * up).astype(BF16)
+            d_hidden = mm(dyQ[at_i, :], WC[half * HF : (half + 1) * HF, :], NT)
+            d_gate = d_hidden * up * (sigma * (1.0 + gate * (1.0 - sigma)))
+            dgdu[at_i, half * FC : half * FC + HF] = d_gate.astype(BF16)
+            dgdu[at_i, half * FC + HF : (half + 1) * FC] = (d_hidden * silu).astype(BF16)
+
+        loop(T // L, body)
+
+    ffn(0, r)
+    h2_finish()
+    ffn(0, r_sib)
     ag_forward(6)
+    ffn(0, r_par)
+    ffn(0, r_dia)
 
     YS, YR, ZR, QS, QR = (R[k] for k in ("YS", "YR", "ZR", "QS", "QR"))
     y_sem, z_sem = [take(Z) for _ in range(4)], [take(Z - 1) for _ in range(4)]
@@ -718,49 +741,52 @@
         elif unit < 3:
             store(slice(0, FC), mm(h2Q[:, at_g], dgdu[:, (unit - 1) * FC : unit * FC], TN))
         else:
-            store(slice(0, 3 * QC), mm(h1Q[:, at_g], hid[:, 0 : 3 * QC], TN))
+            store(slice(0, 3 * QC), mm(h1Q[:, at_g], WC[:, 0 : 3 * QC], TN))
             store(slice(3 * QC, 4 * QC), mm(attQ[:, at_g], R["daR"][...], TN))
 
+    slots = {1: 0, 2: 1, 0: 2, 3: 0}
+
     def y_copy(unit, i):
-        return remote(YS.at[unit % 2, i], YR.at[unit, i], peer, y_sem[unit] + i)
+        return remote(YS.at[slots[unit], i], YR.at[unit, i], peer, y_sem[unit] + i)
 
     def z_copy(unit, i):
         return remote(YR.at[unit, i], ZR.at[unit, i - 1], z_dev(i), z_sem[unit] + i - 1)
 
-    def order(i):
-        return lax.rem(i + 1, Z)
-
-    def rs_first(unit):
-        if unit >= 2:
+    def order(unit, i):
+        return lax.rem(i + Z - z, Z) if unit == 0 else (i + 1) % Z if isinstance(i, int) else lax.rem(i + 1, Z)
+
+    def rs_first(unit, begin=0, count=Z, send=True):
+        if unit == 3:
             for i in range(Z):
-                y_copy(unit - 2, i).wait_send()
+                y_copy(1, i).wait_send()
 
         def body(i):
-            d = order(i)
+            d = order(unit, begin + i)
 
             def store(cols, value):
-                YS[unit % 2, d, :, cols] = value.astype(BF16)
+                YS[slots[unit], d, :, cols] = value.astype(BF16)
 
             gradient(unit, 2 * at_z(d) + 1 - y, store)
-            y_copy(unit, d).start()
-
-        loop(Z, body)
-
-    def rs_second(unit):
-        def body(i):
-            d = order(i)
-            y_copy(unit, d).wait_recv()
-
-            def store(cols, value):
-                YR[unit, d, :, cols] = (value + YR[unit, d, :, cols].astype(F32)).astype(BF16)
-
-            gradient(unit, 2 * at_z(d) + y, store)
-
-            @pl.when(d != 0)
-            def _():
-                z_copy(unit, d).start()
-
-        loop(Z, body)
+            if send:
+                y_copy(unit, d).start()
+
+        loop(count, body)
+
+    def rs_step(unit, i):
+        d = order(unit, i)
+        y_copy(unit, d).wait_recv()
+
+        def store(cols, value):
+            YR[unit, d, :, cols] = (value + YR[unit, d, :, cols].astype(F32)).astype(BF16)
+
+        gradient(unit, 2 * at_z(d) + y, store)
+
+        @pl.when(d != 0)
+        def _():
+            z_copy(unit, d).start()
+
+    def rs_second(unit, begin=0, count=Z):
+        loop(count, lambda i: rs_step(unit, begin + i))
 
     quad_copies = {}
 
@@ -786,21 +812,11 @@
     def rs_last(unit):
         for copy in quad_copies[unit]:
             copy.wait_recv()
-        for q in range(4):
-            if unit == 3:
-                for m, name in enumerate(("gq", "gk", "gv", "go")):
-                    R[name][:, QC * q : QC * (q + 1)] = QR[unit - 1, q, :, QC * m : QC * (m + 1)].astype(F32)
-            else:
-                for j in range(G):
-                    half, within = divmod(B * j, HF)
-                    if half == unit - 1:
-                        target = slice(B * (4 * j + q), B * (4 * j + q) + B)
-                        R["gg"][:, target] = QR[unit - 1, q, :, within : within + B].astype(F32)
-                        R["gu"][:, target] = QR[unit - 1, q, :, HF + within : HF + within + B].astype(F32)
+        R["parts"][unit - 1] = QR[unit - 1]
 
     rsS, rsR = R["rsS"], R["rsR"]
 
-    def quad_sum(kind, prepare_block, partial):
+    def quad_sum(kind, prepare_block, partial, fill=None):
         width = 512
         tiles = [slice(width * j, width * (j + 1)) for j in range(D // width)]
         copies = [
@@ -835,9 +851,13 @@
         copies[1].wait_recv()
         blocks(r_par, to_par)
         copies[2].start()
+        if fill:
+            fill(0)
         prepare_block(r_sib)
         blocks(r_sib, to_sib)
         copies[0].start()
+        if fill:
+            fill(1)
         prepare_block(r)
         blocks(r, keep)
 
@@ -852,32 +872,22 @@
     def summed(kind, at_i):
         return acc[at_i, :] + (rsR[kind, 0, at_i, :].astype(F32) + rsR[kind, 2, at_i, :].astype(F32))
 
-    rs_first(0)
+    def nothing(role):
+        return None
+
+    rs_first(1, send=False)
     ag_forward(7)
-    rs_second(0)
+    for i in range(Z):
+        y_copy(1, order(1, i)).start()
+    rs_first(0, 0, Z // 2)
     ag_finish(6)
     ag_finish(7)
-
-    def ffn_back(role):
-        def body(i):
-            at_i = at(T * role + L * i, L)
-            for half in range(2):
-                both = mm(h2Q[at_i, :], WB[:, half * FC : (half + 1) * FC])
-                gate, up = both[:, 0:HF], both[:, HF:FC]
-                d_hidden = mm(dyQ[at_i, :], WC[half * HF : (half + 1) * HF, :], NT)
-                sigma = 1.0 / (1.0 + jnp.exp(-gate))
-                d_up = d_hidden * (gate * sigma)
-                d_gate = d_hidden * up * (sigma * (1.0 + gate * (1.0 - sigma)))
-                dgdu[at_i, half * FC : half * FC + HF] = d_gate.astype(BF16)
-                dgdu[at_i, half * FC + HF : (half + 1) * FC] = d_up.astype(BF16)
-
-        loop(T // L, body)
-
-    def nothing(role):
-        return None
-
-    h2_sum = quad_sum(0, ffn_back, lambda at_i, cols: mm(dgdu[at_i, :], WB[cols, :], NT))
-    rs_first(1)
+    h2_sum = quad_sum(
+        0, functools.partial(ffn, 1), lambda at_i, cols: mm(dgdu[at_i, :], WB[cols, :], NT),
+        lambda i: rs_second(1, i, 1),
+    )
+    rs_second(1, 2, 1)
+    rs_first(2)
     h2_sum()
 
     TT, TR = R["TT"], R["TR"]
@@ -912,19 +922,19 @@
         go(copy)
     dattR[at(T * r, T), :] = dattS[:, lanes(QC * r, QC)]
     daR[at(T * r, T), :] = daS[:, lanes(QC * r, QC)]
-    rs_second(1)
-    rs_first(2)
-
+    rs_second(1, 3, 1)
+    rs_first(0, Z // 2, Z // 2)
+    rs_second(0, 0, Z // 2)
     out_sum = quad_sum(1, nothing, lambda at_i, cols: mm(hid[at_i, :], WC[:, cols]))
-    out_sum()
+    for copy in along[2] + along[3] + over[2] + over[3]:
+        copy.wait_send()
+        sent[:] = [other for other in sent if other is not copy]
+    for copy in sendT:
+        copy.wait_recv()
 
     def write_out(i):
         at_i = at(step * i, step)
         R["act"][at_i, :] = (x1[at_i, :] + summed(1, at_i)).astype(BF16)
-
-    loop(T // step, write_out)
-    for copy in sendT:
-        copy.wait_recv()
 
     HG, BG = R["HG"], R["BG"]
     HG[...] = jnp.zeros(HG.shape, F32)
@@ -939,7 +949,7 @@
         d = d * cosine - swap(d) * sine
         inv = lax.rsqrt(per_head(raw * raw) / 64 + EPSILON)
         HG[m, j] += fold(d * (raw * inv))
-        d = d * hgain[m : m + 1, :]
+        d = d * small[2 + m : 3 + m, :]
         return inv * d - raw * (inv * inv * inv * (per_head(d * raw) / 64))
 
     def attend_back(q):
@@ -964,19 +974,26 @@
             d_key = jnp.where(low, dk[0], dk[1])
             d_query = prepare_back(qraw[at_q, tile], d_query, 0, j, cosine, sine, 0.125)
             d_key = prepare_back(kraw[at_q, tile], d_key, 1, j, cosine, sine, 1.0)
-            hid[at_q, tile] = d_query.astype(BF16)
-            hid[at_q, QC + 128 * j : QC + 128 * (j + 1)] = d_key.astype(BF16)
-            hid[at_q, 2 * QC + 128 * j : 2 * QC + 128 * (j + 1)] = jnp.where(low, dv[0], dv[1]).astype(BF16)
-
-    loop(4 * S, attend_back)
-    rs_second(2)
+            WC[at_q, tile] = d_query.astype(BF16)
+            WC[at_q, QC + 128 * j : QC + 128 * (j + 1)] = d_key.astype(BF16)
+            WC[at_q, 2 * QC + 128 * j : 2 * QC + 128 * (j + 1)] = jnp.where(low, dv[0], dv[1]).astype(BF16)
+
+    def attend_and_step(i):
+        for q in range(S):
+            attend_back(S * i + q)
+        rs_step(2, i)
+
+    loop(4, attend_and_step)
     for copy in sendD:
         copy.wait_recv()
     rs_first(3)
-    rs_third(0)
-    in_sum = quad_sum(2, nothing, lambda at_i, cols: mm(hid[at_i, 0 : 3 * QC], WA[cols, 0 : 3 * QC], NT))
+    out_sum()
+    loop(T // step, write_out)
+    in_sum = quad_sum(
+        2, nothing, lambda at_i, cols: mm(WC[at_i, 0 : 3 * QC], WA[cols, 0 : 3 * QC], NT),
+        lambda i: rs_second(0, Z // 2 + i, 1),
+    )
     rs_third(1)
-    rs_second(3)
     in_sum()
 
     def input_back(i):
@@ -991,7 +1008,6 @@
         for j in range(1, QC // 128):
             value = value + HG[m, j]
         TT[0, 2:3, 128 * m : 128 * (m + 1)] = jnp.sum(value, axis=0, keepdims=True)
-    spot = lax.broadcasted_iota(jnp.int32, (1, 128), 1)
     for m in range(2):
         line = jnp.zeros((1, 128), F32)
         for h in range(QC // 64):
@@ -999,39 +1015,82 @@
         TT[0, 3 + m : 4 + m, 0:128] = line
     t1, t2, t3, t_finish = tile_sum(TT, TR)
     t1()
+    rs_second(3, 0, 3)
+    t2()
+    rs_second(3, 3, 1)
     rs_third(2)
-    t2()
     rs_last(1)
     t3()
+    rs_third(0)
+    rs_third(3)
     rs_last(2)
     R["tot"][...] = t_finish()
-    rs_third(3)
     rs_last(3)
     for copy in sent:
         copy.wait_send()
     for unit in range(4):
         for i in range(Z):
-            if unit >= 2:
+            if unit != 1:
                 y_copy(unit, i).wait_send()
             if i:
                 z_copy(unit, i).wait_send()
 
 
+LAST = ("act", "ig", "gq", "gk", "gv", "go", "gg", "gu", "gd", "ga", "gf", "ghq", "ghk", "gb")
+
+
+def finishing(s, *refs):
+    names = tuple(name + "_in" for name in OUTPUTS) + LAST
+    R = dict(zip(names, refs, strict=True))
+    D, rows, G, QC, FC, B, HD, H = (s[k] for k in ("D", "rows", "G", "QC", "FC", "B", "HD", "H"))
+    HF = FC // 2
+    for name in ("act", "ig", "gd"):
+        R[name][...] = R[name + "_in"][...]
+    parts = R["parts_in"]
+    for q in range(4):
+        for m, name in enumerate(("gq", "gk", "gv", "go")):
+            R[name][:, QC * q : QC * (q + 1)] = parts[2, q, :, QC * m : QC * (m + 1)].astype(F32)
+        for j in range(G):
+            half, within = divmod(B * j, HF)
+            target = slice(B * (4 * j + q), B * (4 * j + q) + B)
+            R["gg"][:, target] = parts[half, q, :, within : within + B].astype(F32)
+            R["gu"][:, target] = parts[half, q, :, HF + within : HF + within + B].astype(F32)
+    tot = R["tot_in"]
+    own = lax.axis_index("fsdp") * rows
+    mine = pltpu.roll(tot[:, lanes(128 * lax.div(own, 128), 128)], lax.rem(128 - lax.rem(own, 128), 128), 1)
+    R["ga"][...] = mine[0:1, 0:rows]
+    R["gf"][...] = mine[1:2, 0:rows]
+    both = tot[:, 0:256]
+    both = both + pltpu.roll(both, 256 - HD, 1)
+    R["ghq"][...] = both[2:3, 0:HD]
+    R["ghk"][...] = both[2:3, 128 : 128 + HD]
+    R["gb"][...] = tot[3:5, 0:H]
+
+
 def layer(s, tokens, segment_ids, variate_ids, time_ids, w_query, w_key, w_value, w_out, w_gate, w_up, w_down,
           gain_attn, gain_ffn, gain_query, gain_key, variate_bias, cotangent):
-    D, T, rows, B, FF = s["D"], s["T"], s["rows"], s["B"], s["FF"]
-    owner = lax.axis_index("fsdp")
-    pair = jnp.stack([gain_attn, gain_ffn]).astype(F32)
-    gains = lax.dynamic_update_slice(jnp.zeros((8, D), F32), pair, (0, owner * rows))
-    hgain = jnp.tile(jnp.stack([gain_query, gain_key]).astype(F32), (4, 2))
+    D, T, rows, B, FF, FC, HD, H = (s[k] for k in ("D", "T", "rows", "B", "FF", "FC", "HD", "H"))
+    lines = [
+        gain_attn[None], gain_ffn[None], jnp.tile(gain_query[None], (1, 2)), jnp.tile(gain_key[None], (1, 2)),
+        variate_bias,
+    ]
+    small, line = jnp.zeros((8, 128), F32), 0
+    for piece in lines:
+        high, wide = piece.shape
+        small = small + jnp.pad(piece.astype(F32), ((line, 8 - line - high), (0, 128 - wide)))
+        line += high
     scratch = scratch_of(s)
     names = INPUTS + OUTPUTS + tuple(scratch)
     vmem = pl.BlockSpec(memory_space=pltpu.VMEM)
-    small = [(rows, D)] * 4 + [(rows, FF)] * 2 + [(B, D), (8, D)]
+
+    def shape(*dims, kind=F32):
+        return jax.ShapeDtypeStruct(dims, kind)
+
+    tokens_shape = shape(T, D, kind=BF16)
     outs = pl.pallas_call(
         functools.partial(fused, s, names),
-        out_shape=[jax.ShapeDtypeStruct((T, D), BF16)] * 2 + [jax.ShapeDtypeStruct(d, F32) for d in small],
-        in_specs=[vmem] * (len(INPUTS) - 1) + [pl.BlockSpec(memory_space=pltpu.SMEM)],
+        out_shape=[tokens_shape, tokens_shape, shape(B, D), shape(3, 4, rows, FC, kind=BF16), shape(8, D)],
+        in_specs=[vmem] * len(INPUTS),
         out_specs=[vmem] * len(OUTPUTS),
         scratch_shapes=list(scratch.values()),
         compiler_params=pltpu.CompilerParams(
@@ -1040,17 +1099,18 @@
         name="fused_layer",
     )(
         tokens.reshape(T, D), cotangent.reshape(T, D), segment_ids, variate_ids, time_ids,
-        w_query, w_key, w_value, w_out, w_gate, w_up, w_down, gains, hgain, variate_bias.astype(F32),
-    )
-    act, ig, gq, gk, gv, go, gg, gu, gd, tot = outs
-    attn_own = lax.dynamic_slice(tot, (0, owner * rows), (1, rows)).reshape(rows)
-    ffn_own = lax.dynamic_slice(tot, (1, owner * rows), (1, rows)).reshape(rows)
-    HD, H = s["HD"], s["H"]
-    return (
-        act.reshape(tokens.shape), ig.reshape(tokens.shape), gq, gk, gv, go, gg, gu, gd, attn_own, ffn_own,
-        tot[2, 0:HD] + tot[2, HD : 2 * HD], tot[2, 128 : 128 + HD] + tot[2, 128 + HD : 128 + 2 * HD],
-        tot[3:5, 0:H],
-    )
+        w_query, w_key, w_value, w_out, w_gate, w_up, w_down, small,
+    )
+    last = pl.pallas_call(
+        functools.partial(finishing, s),
+        out_shape=[tokens_shape, tokens_shape] + [shape(rows, D)] * 4 + [shape(rows, FF)] * 2
+        + [shape(B, D), shape(1, rows), shape(1, rows), shape(1, HD), shape(1, HD), shape(2, H)],
+        in_specs=[vmem] * len(OUTPUTS),
+        out_specs=[vmem] * len(LAST),
+        name="finishing",
+    )(*outs)
+    flat = [value.reshape(-1) for value in last[9:13]]
+    return (last[0].reshape(tokens.shape), last[1].reshape(tokens.shape), *last[2:9], *flat, last[13])
 
 
 def local(tokens, segment_ids, variate_ids, time_ids, *rest):

time: 336 us -> 260 us (0.77)
  Pallas kernels: 316 us -> 257 us
  local copies, waits for them, and re-layouts: 15.9 us -> 1.99 us
    pallas_call x1 -> x2, Pallas kernels: 316 us -> 257 us  [the longest x1 253 us: layer(): pl.pallas_call(functools.partial(fused, s, names), out_shape=[tokens_shap...]
    unnamed x35 -> x10, local copies, waits for them, and re-layouts: 10.4 us -> 1.82 us
where the time goes in v2:
time: 260 us
  Pallas kernels  257 us (99%)
    pallas_call x1, Pallas kernels, layer(): pl.pallas_call(functools.partial(fused, s, names), out_shape=[tokens_shap...  253 us

profile of v2, /device:TPU:25, one launch (start us, length us, event | category | flops | bytes accessed | tf_op | source)
XLA Modules:
  0.0 260.2 jit_solution(17179095346210958256)
XLA Ops:
  0.6 0.0 copy-start.3
  0.7 0.6 copy-done.3
  1.3 0.0 copy-start.4
  1.3 0.1 convert_element_type.52
  1.4 0.6 copy-done.4
  2.0 0.0 copy-start
  2.0 0.0 copy-start.1
  2.0 0.0 copy-start.2
  2.0 0.1 convert_element_type.54
  2.1 0.6 copy-done
  2.6 0.0 copy-done.1
  2.6 0.0 copy-done.2
  2.6 0.6 convert_add_fusion.refs_12_
  3.3 253.4 %fused_layer.1 = (bf16[256,1024]{1,0:T(8,128)(2,1)}, bf16[256,1024]{1,0:T(8,128)(2,1)}, f32[128,1024]{1,0:T(8,128)}, bf16[3,4,32,1024]{3,2,1,0:T(8,128)(2,1)}, f32[8,1024]{1,0:T(8,128)}) custom-call(bf16[256,1024]{1,0:T(8,128)(2,1)} %bitcast.10, bf16[256,1024]{1,0:T(8,128)(2,1)} %bitcast.11, s32[2,128]{1,0:T(2,128)} %refs_2_.1, s32[2,128]{1,0:T(2,128)} %refs_3_.1, ...), custom_call_target="tpu_custom_call" | custom-call | tf_op jit(solution)/shard_map/fused_layer/pallas_call | solution.py:1090
  256.7 3.3 %finishing.1 = (bf16[256,1024]{1,0:T(8,128)(2,1)}, bf16[256,1024]{1,0:T(8,128)(2,1)}, f32[32,1024]{1,0:T(8,128)}, f32[32,1024]{1,0:T(8,128)}, f32[32,1024]{1,0:T...) custom-call(bf16[256,1024]{1,0:T(8,128)(2,1)} %get-tuple-element.33., ...), custom_call_target="tpu_custom_call" | custom-call | tf_op jit(solution)/shard_map/finishing/pallas_call | solution.py:1104
  (2 shorter events, 0.0 us)
Async XLA Ops:
  0.6 0.7 copy-start.3
  1.3 0.7 copy-start.4
  2.0 0.7 copy-start
  2.0 0.7 copy-start.1
  2.0 0.7 copy-start.2

commit v3 on v2

--- a/solution.py
+++ b/solution.py
@@ -349,7 +349,7 @@
     return (
         s["n"] % 8 == 0 and s["rows"] % 16 == 0 and s["L"] == 128 and s["HD"] == 64
         and s["H"] * s["HD"] == s["D"] and s["QC"] % 128 == 0 and s["FF"] == 4 * s["D"]
-        and s["B"] % 128 == 0 and s["FC"] // 2 % s["B"] == 0 and s["FC"] == s["D"]
+        and s["B"] == 128 and s["FC"] // 2 % s["B"] == 0 and s["FC"] == s["D"]
     )
 
 
@@ -370,10 +370,11 @@
         hid=vm((Q, FC), BF16), dgdu=vm((Q, 2 * FC), BF16),
         rsS=vm((3, T, D), BF16), rsR=vm((3, 3, T, D), BF16),
         daS=vm((T, D), BF16), daR=vm((Q, QC), BF16), dattS=vm((T, D), BF16), dattR=vm((Q, QC), BF16),
-        YS=vm((3, Z, B, FC), BF16), YR=vm((4, Z, B, FC), BF16), ZR=vm((4, Z - 1, B, FC), BF16),
+        YS=vm((3, Z, B, FC), BF16), YR=vm((4, Z, B, FC), BF16), ZR=vm((4, Z - 1, B, FC), BF16), ZX=vm((4, B, FC), BF16),
         QS=vm((3, B, FC), BF16), QR=vm((3, 4, rows, FC), BF16),
         idq=vm((4 * S, 8, L), F32),
-        GT=vm((3, 8, D), F32), GR=vm((4 + Z, 8, D), F32),
+        SW=vm((4, rows, D), BF16), SG=vm((2, rows, s["FF"]), BF16), TK=vm((T, D), BF16),
+        GQ=vm((4, 8, B), F32), GA=vm((8, D), F32), load=pltpu.SemaphoreType.DMA((9,)),
         TT=vm((3, 8, D), F32), TR=vm((4 + Z, 8, D), F32),
         HG=vm((4, QC // 128, 8, 128), F32), BG=vm((2, QC // 64, 8, 128), F32),
         send=pltpu.SemaphoreType.DMA((192,)), recv=pltpu.SemaphoreType.DMA((192,)),
@@ -411,6 +412,15 @@
     def z_src(step):
         return lax.rem(z + Z - step, Z)
 
+    relays = Z == 4
+    inner, outer = lax.rem(z + 1, 4) >= 2, lax.rem(z + 1, 4) < 2
+
+    def nearby(step, action):
+        if relays and step != 2:
+            pl.when(z != (Z - 1 if step == 1 else 0))(action)
+        else:
+            action()
+
     used = [0]
     sent = []
 
@@ -418,10 +428,11 @@
         used[0] += count
         return used[0] - count
 
-    def remote(src, dst, device, sem=None):
+    def remote(src, dst, device, sem=None, arrival=None):
         sem = take() if sem is None else sem
+        arrival = sem if arrival is None else arrival
         return pltpu.make_async_remote_copy(
-            src_ref=src, dst_ref=dst, send_sem=R["send"].at[sem], recv_sem=R["recv"].at[sem],
+            src_ref=src, dst_ref=dst, send_sem=R["send"].at[sem], recv_sem=R["recv"].at[arrival],
             device_id=(device,), device_id_type=MESH,
         )
 
@@ -430,36 +441,32 @@
         sent.append(copy)
         return copy
 
-    SA, SB, WA, WB, WC, WO = (R[k] for k in ("SA", "SB", "WA", "WB", "WC", "WO"))
-    for q in range(4):
-        for m, name in enumerate(("wq", "wk", "wv", "wo")):
-            SA[q, :, QC * m : QC * (m + 1)] = R[name][:, QC * q : QC * (q + 1)]
-        for j in range(G):
-            half, within = divmod(B * j, HF)
-            source = slice(B * (4 * j + q), B * (4 * j + q) + B)
-            SB[q, :, half * FC + within : half * FC + within + B] = R["wg"][:, source]
-            SB[q, :, half * FC + HF + within : half * FC + HF + within + B] = R["wu"][:, source]
+    barrier = pltpu.get_barrier_semaphore()
+    others = [sib, par, dia, peer] + [z_dev(d) for d in range(1, Z)]
+    for device in others:
+        pl.semaphore_signal(barrier, inc=1, device_id=(device,), device_id_type=MESH)
+
+    SA, SB, SW, SG, WA, WB, WC, WO = (R[k] for k in ("SA", "SB", "SW", "SG", "WA", "WB", "WC", "WO"))
+    dyQ, h1Q, h2Q, attQ, tok = R["dyQ"], R["h1Q"], R["h2Q"], R["attQ"], R["TK"]
+    places = [("wq", SW.at[0]), ("wk", SW.at[1]), ("wv", SW.at[2]), ("wo", SW.at[3]), ("wd", WC.at[at(B * g, B)])]
+    places += [("tok", tok), ("wg", SG.at[0]), ("wu", SG.at[1]), ("cot", dyQ.at[at(T * r, T)])]
+    loads = {}
+    for i, (name, place) in enumerate(places):
+        loads[name] = pltpu.make_async_copy(R[name], place, R["load"].at[i])
+        loads[name].start()
     own = at(B * g + rows * r, rows)
-    WA[own, :] = SA[r]
-    WB[own, :] = SB[r]
-    WC[at(B * g, B), :] = R["wd"][...]
-    idq = R["idq"]
+    idq, small, GQ, GA = R["idq"], R["small"], R["GQ"], R["GA"]
     for q in range(S):
         idq[S * r + q, 0:1, :] = R["seg"][q : q + 1, :].astype(F32)
         idq[S * r + q, 1:2, :] = R["var"][q : q + 1, :].astype(F32)
         idq[S * r + q, 2:3, :] = R["tim"][q : q + 1, :].astype(F32)
         idq[S * r + q, 3:8, :] = jnp.zeros((5, L), F32)
-    GT, GR = R["GT"], R["GR"]
-    small = R["small"]
-    GT[0] = jnp.zeros((8, D), F32)
-    GT[0, :, lanes(128 * lax.div(rows * me, 128), 128)] = pltpu.roll(small[...], lax.rem(rows * me, 128), 1)
-    dyQ, h1Q, h2Q, attQ = R["dyQ"], R["h1Q"], R["h2Q"], R["attQ"]
-    dyQ[at(T * r, T), :] = R["cot"][...]
-
-    barrier = pltpu.get_barrier_semaphore()
-    others = [sib, par, dia, peer] + [z_dev(d) for d in range(1, Z)]
-    for device in others:
-        pl.semaphore_signal(barrier, inc=1, device_id=(device,), device_id_type=MESH)
+    GQ[r] = pltpu.roll(small[...], rows * r, 1)
+    for m, name in enumerate(("wq", "wk", "wv", "wo")):
+        loads[name].wait()
+        for q in range(4):
+            SA[q, :, QC * m : QC * (m + 1)] = SW[m, :, QC * q : QC * (q + 1)]
+    WA[own, :] = SA[r]
     pl.semaphore_wait(barrier, len(others))
 
     def tile_sum(tile, got):
@@ -514,53 +521,101 @@
         return start, forward, finish
 
     chunks = [(WA, 0, 2 * QC), (WA, 2 * QC, 2 * QC), (WC, 0, D // 2), (WC, D // 2, D // 2)]
-    chunks += [(WB, HF * k, HF) for k in range(4)]
+    chunks += [(WB, HF * k, HF) for k in range(4)] + [(GA, 0, B)]
+    early, after = 3, {0: 2, 2: 4, 3: 5, 4: 6, 5: 7}
 
     def piece(k, group):
         ref, start, size = chunks[k]
+        if ref is GA:
+            return ref.at[:, lanes(B * group, B)]
         return ref.at[at(B * group, B), pl.ds(start, size)]
 
-    along = [[remote(piece(k, g), piece(k, g), z_dev(d)) for d in range(1, Z)] for k in range(8)]
-    over = [
-        [remote(piece(k, 2 * z_src(d) + y), piece(k, 2 * z_src(d) + y), peer) for d in range(Z)]
-        for k in range(8)
-    ]
+    a_sem, f_sem, o_sem = ([take(size) for _ in chunks] for size in (Z - 1, 1, Z))
+    b_sem, e_sem = take(Z - 1), take()
+
+    def across_y(other):
+        return y + other * (1 - 2 * y)
+
+    def along(k, d, other=0):
+        block = piece(k, 2 * z + across_y(other))
+        return remote(block, block, z_dev(d), (b_sem if other else a_sem[k]) + d - 1)
+
+    def over(k, d):
+        block = piece(k, 2 * z_src(d) + y)
+        return remote(block, block, peer, o_sem[k] + d)
+
+    def relay(k, other=0):
+        block, end = piece(k, 2 * z_src(2) + across_y(other)), lax.div(z, 2)
+        sems = (e_sem, b_sem + 2 * end) if other else (f_sem[k], a_sem[k] + 2 * end)
+        return remote(block, block, 3 * end * 8 + y * 4 + r, *sems)
+
+    def near(k, d, action):
+        if k == 8:
+            action()
+        else:
+            nearby(d, action)
+
+    def both(k):
+        return (0, 1) if k == early else (0,)
 
     def ag_start(k):
-        for copy in along[k]:
-            go(copy)
+        for other in both(k):
+            for d in range(1, Z):
+                near(k, d, along(k, d, other).start)
 
     def ag_own(k):
-        go(over[k][0])
+        over(k, 0).start()
 
     def ag_forward(k):
-        for d in range(1, Z):
-            along[k][d - 1].wait_recv()
-            go(over[k][d])
-        if k + 2 < len(chunks):
-            ag_own(k + 2)
+        first = lax.div(3 - z, 3)
+        for i in range(1, Z):
+            d = i if not relays or i == 2 else 1 + 2 * first if i == 1 else 3 - 2 * first
+            for other in both(k):
+                along(k, d, other).wait_recv()
+                if relays and i == 2 and k < 8:
+                    pl.when(inner)(relay(k, other).start)
+            if k != early:
+                over(k, d).start()
+        if k in after:
+            ag_own(after[k])
+        if 2 <= k <= 4:
+            ag_start(k + 3)
 
     def ag_finish(k):
-        for copy in over[k]:
-            copy.wait_recv()
-
-    g1, g2, g3, g_finish = tile_sum(GT, GR)
-    g1()
+        for d in range(Z):
+            if k != early:
+                over(k, d).wait_recv()
+
+    def ag_drain(k):
+        for d in range(1 if k == early else Z):
+            over(k, d).wait_send()
+        for other in both(k):
+            for d in range(1, Z):
+                near(k, d, along(k, d, other).wait_send)
+            if relays and k < 8:
+                pl.when(inner)(relay(k, other).wait_send)
+
+    sendG = [remote(GQ.at[r], GQ.at[r], dev) for dev, q in quad]
     sendA = [remote(SA.at[q], WA.at[own], dev) for dev, q in quad]
     sendB = [remote(SB.at[q], WB.at[own], dev) for dev, q in quad]
-    for copy in sendA:
-        go(copy)
     mine = idq.at[pl.ds(S * r, S)]
     sendI = [remote(mine, mine, dev) for dev, q in quad]
-    for copy in sendI:
+    for copy in sendG + sendA + sendI:
         go(copy)
-    g2()
+    loads["wd"].wait()
+    ag_own(early)
+    for copy in sendG:
+        copy.wait_recv()
+    GA[:, lanes(B * g, B)] = (GQ[0] + GQ[1]) + (GQ[2] + GQ[3])
+    ag_start(8)
+    ag_own(8)
     for copy in sendA:
         copy.wait_recv()
-    for k in range(4):
-        ag_start(k)
-        if k < 2:
-            ag_own(k)
+    ag_start(0)
+    ag_own(0)
+    ag_start(1)
+    ag_own(1)
+    ag_start(2)
     for copy in sendI:
         copy.wait_recv()
 
@@ -579,19 +634,16 @@
         ST[at(L * q, L), :] = jnp.where(front, -sine, sine)
 
     loop(2 * S, tables)
-    g3()
+    ag_forward(8)
     loop(2 * S, lambda q: tables(2 * S + q))
-    for copy in sent[:3]:
-        copy.wait_send()
-    del sent[:3]
-    GT[0] = g_finish()
-    tok = R["tok"]
+    loads["tok"].wait()
+    ag_finish(8)
     step = 64
 
     def norm_in(i):
         x = tok[at(step * i, step), :].astype(F32)
         inv = lax.rsqrt(jnp.mean(x * x, axis=-1, keepdims=True) + EPSILON)
-        h1Q[at(T * r + step * i, step), :] = (x * inv * GT[0, 0:1, :]).astype(BF16)
+        h1Q[at(T * r + step * i, step), :] = (x * inv * GA[0:1, :]).astype(BF16)
 
     loop(T // step, norm_in)
 
@@ -600,23 +652,44 @@
 
     h1_start, h1_forward, h1_finish = quad_gather(token_block(h1Q))
     dy_start, dy_forward, dy_finish = quad_gather(token_block(dyQ))
-    att_start, att_forward, att_finish = quad_gather(lambda role: attQ.at[:, lanes(QC * role, QC)])
+
+    def att_block(chip, role):
+        return attQ.at[at(2 * T * chip, 2 * T), lanes(QC * role, QC)]
+
+    def att_copy(chip, role, device):
+        return remote(att_block(chip, role), att_block(chip, role), device)
+
+    needed, passed = att_copy(1 - xx, r, par), att_copy(xx, r_par, sib)
+    near_needed, near_rest = att_copy(xx, r, sib), att_copy(1 - xx, r, sib)
+    rest, passed_rest = att_copy(xx, r, par), att_copy(1 - xx, r_par, sib)
     wo_start, wo_forward, wo_finish = quad_gather(lambda role: WO.at[:, lanes(QC * role, QC)])
     h2_start, h2_forward, h2_finish = quad_gather(token_block(h2Q))
     h1_start()
+    for name in ("wg", "wu"):
+        loads[name].wait()
+    for q in range(4):
+        for j in range(G):
+            half, within = divmod(B * j, HF)
+            source = slice(B * (4 * j + q), B * (4 * j + q) + B)
+            SB[q, :, half * FC + within : half * FC + within + B] = SG[0, :, source]
+            SB[q, :, half * FC + HF + within : half * FC + HF + within + B] = SG[1, :, source]
+    WB[own, :] = SB[r]
     for copy in sendB:
         go(copy)
     ag_forward(0)
+    over(early, 0).wait_recv()
+    ag_start(early)
     h1_forward()
     ag_forward(1)
     for copy in sendB:
         copy.wait_recv()
-    for k in range(4, 8):
-        ag_start(k)
+    ag_start(4)
+    loads["cot"].wait()
     dy_start()
     h1_finish()
     ag_finish(0)
     ag_finish(1)
+    ag_forward(2)
 
     qraw, kraw, qr, kr, vb, PR = (R[k] for k in ("qraw", "kraw", "qr", "kr", "vb", "PR"))
     spot = lax.broadcasted_iota(jnp.int32, (1, 128), 1)
@@ -653,7 +726,6 @@
     WO[:, lanes(QC * r, QC)] = WA[:, 3 * QC : 4 * QC]
     wo_start()
     dy_forward()
-    ag_forward(2)
 
     def masks(q):
         segment = jnp.broadcast_to(idq[q, 0:1, :], (L, L))
@@ -680,15 +752,28 @@
                 outs.append(mm(p.astype(BF16), v2))
             attQ[at_q, lanes(QC * r + 128 * j, 128)] = jnp.where(low, outs[0], outs[1]).astype(BF16)
 
-    loop(4 * S, attend)
-    att_start()
+    loop(2 * S, lambda q: attend(2 * S * (1 - xx) + q))
+    go(needed)
     ag_forward(3)
+    loop(2 * S, lambda q: attend(2 * S * xx + q))
+    go(near_needed)
+    go(near_rest)
+    ZR = R["ZR"]
+    if relays:
+        for k, end in ((0, 0), (2, 3)):
+
+            @pl.when(z == end)
+            def _():
+                for unit in range(4):
+                    ZR[unit, k] = jnp.zeros((B, FC), BF16)
+
+    needed.wait_recv()
+    go(passed)
     wo_forward()
     ag_forward(4)
-    att_forward()
     wo_finish()
-    dy_finish()
-    att_finish()
+    near_needed.wait_recv()
+    passed.wait_recv()
 
     x1, dx1, acc = R["x1"], R["dx1"], R["acc"]
 
@@ -696,11 +781,14 @@
         x = tok[at(step * i, step), :].astype(F32) + mm(attQ[at(T * r + step * i, step), :], WO[...])
         x1[at(step * i, step), :] = x
         inv = lax.rsqrt(jnp.mean(x * x, axis=-1, keepdims=True) + EPSILON)
-        h2Q[at(T * r + step * i, step), :] = (x * inv * GT[0, 1:2, :]).astype(BF16)
+        h2Q[at(T * r + step * i, step), :] = (x * inv * GA[1:2, :]).astype(BF16)
 
     loop(T // step, mix)
     h2_start()
+    go(rest)
     ag_forward(5)
+    dy_finish()
+    ag_forward(6)
     ag_finish(2)
     ag_finish(3)
     h2_forward()
@@ -725,14 +813,16 @@
         loop(T // L, body)
 
     ffn(0, r)
+    ag_forward(7)
     h2_finish()
+    rest.wait_recv()
+    go(passed_rest)
     ffn(0, r_sib)
-    ag_forward(6)
     ffn(0, r_par)
     ffn(0, r_dia)
 
-    YS, YR, ZR, QS, QR = (R[k] for k in ("YS", "YR", "ZR", "QS", "QR"))
-    y_sem, z_sem = [take(Z) for _ in range(4)], [take(Z - 1) for _ in range(4)]
+    YS, YR, ZR, ZX, QS, QR = (R[k] for k in ("YS", "YR", "ZR", "ZX", "QS", "QR"))
+    y_sem, z_sem, x_sem = ([take(size) for _ in range(4)] for size in (Z, Z - 1, 1))
 
     def gradient(unit, group, store):
         at_g = lanes(B * group, B)
@@ -749,41 +839,67 @@
     def y_copy(unit, i):
         return remote(YS.at[slots[unit], i], YR.at[unit, i], peer, y_sem[unit] + i)
 
-    def z_copy(unit, i):
-        return remote(YR.at[unit, i], ZR.at[unit, i - 1], z_dev(i), z_sem[unit] + i - 1)
-
-    def order(unit, i):
-        return lax.rem(i + Z - z, Z) if unit == 0 else (i + 1) % Z if isinstance(i, int) else lax.rem(i + 1, Z)
-
-    def rs_first(unit, begin=0, count=Z, send=True):
+    def z_copy(unit, d, i=0):
+        return remote(YR.at[unit, i], ZR.at[unit, d - 1], z_dev(d), z_sem[unit] + d - 1)
+
+    def x_copy(unit, i=0):
+        return remote(YR.at[unit, i], ZX.at[unit], (1 + lax.div(z, 2)) * 8 + y * 4 + r, x_sem[unit])
+
+    def target(unit, i):
+        if not relays:
+            return lax.rem(z + 1 + i, Z)
+        even = 1 - lax.rem(z, 2)
+        if unit == 0:
+            return i + even * (1 - 2 * (i % 2 if isinstance(i, int) else lax.rem(i, 2)))
+        o = (2 * i) % 3 + 3 * (i // 3) if isinstance(i, int) else lax.rem(2 * i, 3) + 3 * lax.div(i, 3)
+        return o + even * (3 - 2 * o)
+
+    def own_place(unit):
+        if not relays:
+            return Z - 1
+        return 1 + 2 * lax.div(z, 2) if unit == 0 else 3 - lax.div(z * (3 - z), 2)
+
+    def rs_first(unit, begin=0, count=Z):
         if unit == 3:
             for i in range(Z):
                 y_copy(1, i).wait_send()
 
         def body(i):
-            d = order(unit, begin + i)
+            place = begin + i
 
             def store(cols, value):
-                YS[slots[unit], d, :, cols] = value.astype(BF16)
-
-            gradient(unit, 2 * at_z(d) + 1 - y, store)
-            if send:
-                y_copy(unit, d).start()
+                YS[slots[unit], place, :, cols] = value.astype(BF16)
+
+            gradient(unit, 2 * target(unit, place) + 1 - y, store)
+            y_copy(unit, place).start()
 
         loop(count, body)
 
     def rs_step(unit, i):
-        d = order(unit, i)
-        y_copy(unit, d).wait_recv()
+        goal = target(unit, i)
+        d = lax.rem(goal + Z - z, Z)
+        y_copy(unit, i).wait_recv()
 
         def store(cols, value):
-            YR[unit, d, :, cols] = (value + YR[unit, d, :, cols].astype(F32)).astype(BF16)
-
-        gradient(unit, 2 * at_z(d) + y, store)
-
-        @pl.when(d != 0)
-        def _():
-            z_copy(unit, d).start()
+            YR[unit, i, :, cols] = (value + YR[unit, i, :, cols].astype(F32)).astype(BF16)
+
+        gradient(unit, 2 * goal + y, store)
+        if not relays:
+            pl.when(d != 0)(lambda: z_copy(unit, d, i).start())
+            return
+        far = outer & (goal + z == 3)
+        pl.when(far)(lambda: x_copy(unit, i).start())
+        pl.when((d != 0) & jnp.logical_not(far | (inner & (d == 2))))(lambda: z_copy(unit, d, i).start())
+
+    def rs_relay(unit):
+        i = 5 - 2 * z if unit == 0 else 3
+        if relays:
+
+            @pl.when(inner)
+            def _():
+                x_copy(unit).wait_recv()
+                YR[unit, i] = (YR[unit, i].astype(F32) + ZX[unit].astype(F32)).astype(BF16)
+                z_copy(unit, 2, i).start()
 
     def rs_second(unit, begin=0, count=Z):
         loop(count, lambda i: rs_step(unit, begin + i))
@@ -791,12 +907,15 @@
     quad_copies = {}
 
     def rs_third(unit):
-        for i in range(1, Z):
-            z_copy(unit, i).wait_recv()
+        for d in range(1, Z):
+            if relays and d != 2:
+                pl.when(z != (0 if d == 1 else Z - 1))(z_copy(unit, d).wait_recv)
+            else:
+                z_copy(unit, d).wait_recv()
         width = 256
         for j in range(FC // width):
             cols = slice(width * j, width * (j + 1))
-            value = YR[unit, 0, :, cols].astype(F32)
+            value = YR[unit, own_place(unit), :, cols].astype(F32)
             for i in range(1, Z):
                 value = value + ZR[unit, i - 1, :, cols].astype(F32)
             if unit == 0:
@@ -875,10 +994,7 @@
     def nothing(role):
         return None
 
-    rs_first(1, send=False)
-    ag_forward(7)
-    for i in range(Z):
-        y_copy(1, order(1, i)).start()
+    rs_first(1)
     rs_first(0, 0, Z // 2)
     ag_finish(6)
     ag_finish(7)
@@ -902,8 +1018,8 @@
 
     def mix_back(i):
         at_i = at(step * i, step)
-        d = norm_back(x1[at_i, :], summed(0, at_i), GT[0, 1:2, :], 1)
-        d = d + R["cot"][at_i, :].astype(F32)
+        d = norm_back(x1[at_i, :], summed(0, at_i), GA[1:2, :], 1)
+        d = d + dyQ[at(T * r + step * i, step), :].astype(F32)
         dx1[at_i, :] = d
         daS[at_i, :] = d.astype(BF16)
 
@@ -924,11 +1040,11 @@
     daR[at(T * r, T), :] = daS[:, lanes(QC * r, QC)]
     rs_second(1, 3, 1)
     rs_first(0, Z // 2, Z // 2)
+    rs_relay(1)
     rs_second(0, 0, Z // 2)
     out_sum = quad_sum(1, nothing, lambda at_i, cols: mm(hid[at_i, :], WC[:, cols]))
-    for copy in along[2] + along[3] + over[2] + over[3]:
-        copy.wait_send()
-        sent[:] = [other for other in sent if other is not copy]
+    ag_drain(2)
+    ag_drain(3)
     for copy in sendT:
         copy.wait_recv()
 
@@ -984,21 +1100,23 @@
         rs_step(2, i)
 
     loop(4, attend_and_step)
-    for copy in sendD:
+    for copy in sendD + [near_rest, passed_rest]:
         copy.wait_recv()
     rs_first(3)
+    rs_relay(2)
     out_sum()
     loop(T // step, write_out)
     in_sum = quad_sum(
         2, nothing, lambda at_i, cols: mm(WC[at_i, 0 : 3 * QC], WA[cols, 0 : 3 * QC], NT),
         lambda i: rs_second(0, Z // 2 + i, 1),
     )
+    rs_relay(0)
     rs_third(1)
     in_sum()
 
     def input_back(i):
         at_i = at(step * i, step)
-        d = norm_back(tok[at_i, :].astype(F32), summed(2, at_i), GT[0, 0:1, :], 0)
+        d = norm_back(tok[at_i, :].astype(F32), summed(2, at_i), GA[0:1, :], 0)
         R["ig"][at_i, :] = (dx1[at_i, :] + d).astype(BF16)
 
     loop(T // step, input_back)
@@ -1018,6 +1136,7 @@
     rs_second(3, 0, 3)
     t2()
     rs_second(3, 3, 1)
+    rs_relay(3)
     rs_third(2)
     rs_last(1)
     t3()
@@ -1028,12 +1147,17 @@
     rs_last(3)
     for copy in sent:
         copy.wait_send()
+    for k in range(len(chunks)):
+        if k not in (2, 3):
+            ag_drain(k)
     for unit in range(4):
         for i in range(Z):
             if unit != 1:
                 y_copy(unit, i).wait_send()
             if i:
-                z_copy(unit, i).wait_send()
+                nearby(i, z_copy(unit, i).wait_send)
+        if relays:
+            pl.when(outer)(x_copy(unit).wait_send)
 
 
 LAST = ("act", "ig", "gq", "gk", "gv", "go", "gg", "gu", "gd", "ga", "gf", "ghq", "ghk", "gb")
@@ -1081,7 +1205,8 @@
         line += high
     scratch = scratch_of(s)
     names = INPUTS + OUTPUTS + tuple(scratch)
-    vmem = pl.BlockSpec(memory_space=pltpu.VMEM)
+    vmem, anywhere = pl.BlockSpec(memory_space=pltpu.VMEM), pl.BlockSpec(memory_space=pl.ANY)
+    here = {"seg", "var", "tim", "small"}
 
     def shape(*dims, kind=F32):
         return jax.ShapeDtypeStruct(dims, kind)
@@ -1090,7 +1215,7 @@
     outs = pl.pallas_call(
         functools.partial(fused, s, names),
         out_shape=[tokens_shape, tokens_shape, shape(B, D), shape(3, 4, rows, FC, kind=BF16), shape(8, D)],
-        in_specs=[vmem] * len(INPUTS),
+        in_specs=[vmem if name in here else anywhere for name in INPUTS],
         out_specs=[vmem] * len(OUTPUTS),
         scratch_shapes=list(scratch.values()),
         compiler_params=pltpu.CompilerParams(

time: 260 us -> 235 us (0.904)
  Pallas kernels: 257 us -> 231 us
    pallas_call x1, Pallas kernels: 253 us -> 228 us  [layer(): pl.pallas_call(functools.partial(fused, s, names), out_shape=[tokens_shap...]
where the time goes in v3:
time: 235 us
  Pallas kernels  231 us (98%)
    pallas_call x1, Pallas kernels, layer(): pl.pallas_call(functools.partial(fused, s, names), out_shape=[tokens_shap...  228 us

profile of v3, /device:TPU:25, one launch (start us, length us, event | category | flops | bytes accessed | tf_op | source)
XLA Modules:
  0.0 234.7 jit_solution(763930486241122451)
XLA Ops:
  0.6 0.0 copy-start.3
  0.7 0.6 copy-done.3
  1.3 0.0 copy-start.4
  1.3 0.1 convert_element_type.52
  1.4 0.6 copy-done.4
  2.0 0.0 copy-start
  2.0 0.0 copy-start.1
  2.0 0.0 copy-start.2
  2.0 0.1 convert_element_type.54
  2.1 0.6 copy-done
  2.6 0.0 copy-done.1
  2.6 0.0 copy-done.2
  2.6 0.6 convert_add_fusion.refs_12_
  3.3 227.9 %fused_layer.1 = (bf16[256,1024]{1,0:T(8,128)(2,1)}, bf16[256,1024]{1,0:T(8,128)(2,1)}, f32[128,1024]{1,0:T(8,128)}, bf16[3,4,32,1024]{3,2,1,0:T(8,128)(2,1)}, f32[8,1024]{1,0:T(8,128)}) custom-call(bf16[256,1024]{1,0:T(8,128)(2,1)} %bitcast.10, bf16[256,1024]{1,0:T(8,128)(2,1)} %bitcast.11, s32[2,128]{1,0:T(2,128)} %refs_2_.1, s32[2,128]{1,0:T(2,128)} %refs_3_.1, ...), custom_call_target="tpu_custom_call" | custom-call | tf_op jit(solution)/shard_map/fused_layer/pallas_call | solution.py:1215
  231.1 3.3 %finishing.1 = (bf16[256,1024]{1,0:T(8,128)(2,1)}, bf16[256,1024]{1,0:T(8,128)(2,1)}, f32[32,1024]{1,0:T(8,128)}, f32[32,1024]{1,0:T(8,128)}, f32[32,1024]{1,0:T...) custom-call(bf16[256,1024]{1,0:T(8,128)(2,1)} %get-tuple-element.33., ...), custom_call_target="tpu_custom_call" | custom-call | tf_op jit(solution)/shard_map/finishing/pallas_call | solution.py:1229
  (2 shorter events, 0.0 us)
Async XLA Ops:
  0.6 0.7 copy-start.3
  1.3 0.7 copy-start.4
  2.0 0.7 copy-start
  2.0 0.7 copy-start.1
  2.0 0.7 copy-start.2

commit v4 on v3

--- a/solution.py
+++ b/solution.py
@@ -522,7 +522,7 @@
 
     chunks = [(WA, 0, 2 * QC), (WA, 2 * QC, 2 * QC), (WC, 0, D // 2), (WC, D // 2, D // 2)]
     chunks += [(WB, HF * k, HF) for k in range(4)] + [(GA, 0, B)]
-    early, after = 3, {0: 2, 2: 4, 3: 5, 4: 6, 5: 7}
+    early, after = 99, {0: 2, 1: 3, 2: 4, 3: 5, 4: 6, 5: 7}
 
     def piece(k, group):
         ref, start, size = chunks[k]
@@ -578,8 +578,8 @@
                 over(k, d).start()
         if k in after:
             ag_own(after[k])
-        if 2 <= k <= 4:
-            ag_start(k + 3)
+        if 2 <= k <= 5:
+            ag_start(k + 2)
 
     def ag_finish(k):
         for d in range(Z):
@@ -603,7 +603,6 @@
     for copy in sendG + sendA + sendI:
         go(copy)
     loads["wd"].wait()
-    ag_own(early)
     for copy in sendG:
         copy.wait_recv()
     GA[:, lanes(B * g, B)] = (GQ[0] + GQ[1]) + (GQ[2] + GQ[3])
@@ -615,7 +614,6 @@
     ag_own(0)
     ag_start(1)
     ag_own(1)
-    ag_start(2)
     for copy in sendI:
         copy.wait_recv()
 
@@ -677,13 +675,12 @@
     for copy in sendB:
         go(copy)
     ag_forward(0)
-    over(early, 0).wait_recv()
-    ag_start(early)
+    ag_start(2)
     h1_forward()
     ag_forward(1)
+    ag_start(3)
     for copy in sendB:
         copy.wait_recv()
-    ag_start(4)
     loads["cot"].wait()
     dy_start()
     h1_finish()
@@ -1111,6 +1108,9 @@
         lambda i: rs_second(0, Z // 2 + i, 1),
     )
     rs_relay(0)
+    for k in range(len(chunks)):
+        if k not in (2, 3):
+            ag_drain(k)
     rs_third(1)
     in_sum()
 
@@ -1147,9 +1147,6 @@
     rs_last(3)
     for copy in sent:
         copy.wait_send()
-    for k in range(len(chunks)):
-        if k not in (2, 3):
-            ag_drain(k)
     for unit in range(4):
         for i in range(Z):
             if unit != 1:

time: 235 us -> 229 us (0.974)
  Pallas kernels: 231 us -> 225 us
    pallas_call x1, Pallas kernels: 228 us -> 221 us  [layer(): pl.pallas_call(functools.partial(fused, s, names), out_shape=[tokens_shap...]
where the time goes in v4:
time: 229 us; the launch traced here: 228 us
  Pallas kernels  225 us (98%)
    pallas_call x1, Pallas kernels, layer(): pl.pallas_call(functools.partial(fused, s, names), out_shape=[tokens_shap...  221 us

profile of v4, /device:TPU:25, one launch (start us, length us, event | category | flops | bytes accessed | tf_op | source)
XLA Modules:
  0.0 228.2 jit_solution(12573484457324578190)
XLA Ops:
  0.6 0.0 copy-start.3
  0.7 0.6 copy-done.3
  1.3 0.0 copy-start.4
  1.3 0.1 convert_element_type.52
  1.4 0.6 copy-done.4
  2.0 0.0 copy-start
  2.0 0.0 copy-start.1
  2.0 0.0 copy-start.2
  2.0 0.1 convert_element_type.54
  2.1 0.6 copy-done
  2.6 0.0 copy-done.1
  2.6 0.0 copy-done.2
  2.6 0.6 convert_add_fusion.refs_12_
  3.3 221.4 %fused_layer.1 = (bf16[256,1024]{1,0:T(8,128)(2,1)}, bf16[256,1024]{1,0:T(8,128)(2,1)}, f32[128,1024]{1,0:T(8,128)}, bf16[3,4,32,1024]{3,2,1,0:T(8,128)(2,1)}, f32[8,1024]{1,0:T(8,128)}) custom-call(bf16[256,1024]{1,0:T(8,128)(2,1)} %bitcast.10, bf16[256,1024]{1,0:T(8,128)(2,1)} %bitcast.11, s32[2,128]{1,0:T(2,128)} %refs_2_.1, s32[2,128]{1,0:T(2,128)} %refs_3_.1, ...), custom_call_target="tpu_custom_call" | custom-call | tf_op jit(solution)/shard_map/fused_layer/pallas_call | solution.py:1212
  224.7 3.3 %finishing.1 = (bf16[256,1024]{1,0:T(8,128)(2,1)}, bf16[256,1024]{1,0:T(8,128)(2,1)}, f32[32,1024]{1,0:T(8,128)}, f32[32,1024]{1,0:T(8,128)}, f32[32,1024]{1,0:T...) custom-call(bf16[256,1024]{1,0:T(8,128)(2,1)} %get-tuple-element.33., ...), custom_call_target="tpu_custom_call" | custom-call | tf_op jit(solution)/shard_map/finishing/pallas_call | solution.py:1226
  (2 shorter events, 0.0 us)
Async XLA Ops:
  0.6 0.7 copy-start.3
  1.3 0.7 copy-start.4
  2.0 0.7 copy-start
  2.0 0.7 copy-start.1
  2.0 0.7 copy-start.2

commit v5 on v4

--- a/solution.py
+++ b/solution.py
@@ -371,6 +371,8 @@
         rsS=vm((3, T, D), BF16), rsR=vm((3, 3, T, D), BF16),
         daS=vm((T, D), BF16), daR=vm((Q, QC), BF16), dattS=vm((T, D), BF16), dattR=vm((Q, QC), BF16),
         YS=vm((3, Z, B, FC), BF16), YR=vm((4, Z, B, FC), BF16), ZR=vm((4, Z - 1, B, FC), BF16), ZX=vm((4, B, FC), BF16),
+        FS=vm((Z, 2, B, FC // 2), BF16), FR=vm((Z - 1, 2, B, FC // 2), BF16), FX=vm((2, B, FC // 2), BF16),
+        FT=vm((2, B, FC // 2), BF16), FK=vm((B, FC // 2), F32),
         QS=vm((3, B, FC), BF16), QR=vm((3, 4, rows, FC), BF16),
         idq=vm((4 * S, 8, L), F32),
         SW=vm((4, rows, D), BF16), SG=vm((2, rows, s["FF"]), BF16), TK=vm((T, D), BF16),
@@ -522,7 +524,7 @@
 
     chunks = [(WA, 0, 2 * QC), (WA, 2 * QC, 2 * QC), (WC, 0, D // 2), (WC, D // 2, D // 2)]
     chunks += [(WB, HF * k, HF) for k in range(4)] + [(GA, 0, B)]
-    early, after = 99, {0: 2, 1: 3, 2: 4, 3: 5, 4: 6, 5: 7}
+    early, after = 7, {0: 2, 1: 3, 2: 4, 3: 5, 4: 6}
 
     def piece(k, group):
         ref, start, size = chunks[k]
@@ -578,8 +580,8 @@
                 over(k, d).start()
         if k in after:
             ag_own(after[k])
-        if 2 <= k <= 5:
-            ag_start(k + 2)
+        if 2 <= k <= 4:
+            ag_start(k + 3)
 
     def ag_finish(k):
         for d in range(Z):
@@ -614,55 +616,6 @@
     ag_own(0)
     ag_start(1)
     ag_own(1)
-    for copy in sendI:
-        copy.wait_recv()
-
-    lane = lax.broadcasted_iota(jnp.int32, (L, 128), 1)
-    sub = lax.broadcasted_iota(jnp.int32, (L, 128), 0)
-    front = lax.rem(lane, 64) < 32
-    low = lane < 64
-    freq = jnp.exp(-math.log(10000.0) * lax.rem(lane, 32).astype(F32) / 32)
-    CT, ST = R["CT"], R["ST"]
-
-    def tables(q):
-        times = jnp.broadcast_to(idq[q, 2:3, :], (L, L)).T
-        angles = times * freq
-        CT[at(L * q, L), :] = jnp.cos(angles)
-        sine = jnp.sin(angles)
-        ST[at(L * q, L), :] = jnp.where(front, -sine, sine)
-
-    loop(2 * S, tables)
-    ag_forward(8)
-    loop(2 * S, lambda q: tables(2 * S + q))
-    loads["tok"].wait()
-    ag_finish(8)
-    step = 64
-
-    def norm_in(i):
-        x = tok[at(step * i, step), :].astype(F32)
-        inv = lax.rsqrt(jnp.mean(x * x, axis=-1, keepdims=True) + EPSILON)
-        h1Q[at(T * r + step * i, step), :] = (x * inv * GA[0:1, :]).astype(BF16)
-
-    loop(T // step, norm_in)
-
-    def token_block(ref):
-        return lambda role: ref.at[at(T * role, T)]
-
-    h1_start, h1_forward, h1_finish = quad_gather(token_block(h1Q))
-    dy_start, dy_forward, dy_finish = quad_gather(token_block(dyQ))
-
-    def att_block(chip, role):
-        return attQ.at[at(2 * T * chip, 2 * T), lanes(QC * role, QC)]
-
-    def att_copy(chip, role, device):
-        return remote(att_block(chip, role), att_block(chip, role), device)
-
-    needed, passed = att_copy(1 - xx, r, par), att_copy(xx, r_par, sib)
-    near_needed, near_rest = att_copy(xx, r, sib), att_copy(1 - xx, r, sib)
-    rest, passed_rest = att_copy(xx, r, par), att_copy(1 - xx, r_par, sib)
-    wo_start, wo_forward, wo_finish = quad_gather(lambda role: WO.at[:, lanes(QC * role, QC)])
-    h2_start, h2_forward, h2_finish = quad_gather(token_block(h2Q))
-    h1_start()
     for name in ("wg", "wu"):
         loads[name].wait()
     for q in range(4):
@@ -674,13 +627,64 @@
     WB[own, :] = SB[r]
     for copy in sendB:
         go(copy)
+    for copy in sendI:
+        copy.wait_recv()
+
+    lane = lax.broadcasted_iota(jnp.int32, (L, 128), 1)
+    sub = lax.broadcasted_iota(jnp.int32, (L, 128), 0)
+    front = lax.rem(lane, 64) < 32
+    low = lane < 64
+    freq = jnp.exp(-math.log(10000.0) * lax.rem(lane, 32).astype(F32) / 32)
+    CT, ST = R["CT"], R["ST"]
+
+    def tables(q):
+        times = jnp.broadcast_to(idq[q, 2:3, :], (L, L)).T
+        angles = times * freq
+        CT[at(L * q, L), :] = jnp.cos(angles)
+        sine = jnp.sin(angles)
+        ST[at(L * q, L), :] = jnp.where(front, -sine, sine)
+
+    loop(2 * S, tables)
+    ag_forward(8)
+    loop(2 * S, lambda q: tables(2 * S + q))
+    loads["tok"].wait()
+    ag_finish(8)
+    step = 64
+
+    def norm_in(i):
+        x = tok[at(step * i, step), :].astype(F32)
+        inv = lax.rsqrt(jnp.mean(x * x, axis=-1, keepdims=True) + EPSILON)
+        h1Q[at(T * r + step * i, step), :] = (x * inv * GA[0:1, :]).astype(BF16)
+
+    loop(T // step, norm_in)
+
+    def token_block(ref):
+        return lambda role: ref.at[at(T * role, T)]
+
+    h1_start, h1_forward, h1_finish = quad_gather(token_block(h1Q))
+    dy_start, dy_forward, dy_finish = quad_gather(token_block(dyQ))
+
+    def att_block(chip, role):
+        return attQ.at[at(2 * T * chip, 2 * T), lanes(QC * role, QC)]
+
+    def att_copy(chip, role, device):
+        return remote(att_block(chip, role), att_block(chip, role), device)
+
+    needed, passed = att_copy(1 - xx, r, par), att_copy(xx, r_par, sib)
+    near_needed, near_rest = att_copy(xx, r, sib), att_copy(1 - xx, r, sib)
+    rest, passed_rest = att_copy(xx, r, par), att_copy(1 - xx, r_par, sib)
+    wo_start, wo_forward, wo_finish = quad_gather(lambda role: WO.at[:, lanes(QC * role, QC)])
+    h2_start, h2_forward, h2_finish = quad_gather(token_block(h2Q))
+    h1_start()
+    for copy in sendB:
+        copy.wait_recv()
+    ag_own(early)
     ag_forward(0)
     ag_start(2)
     h1_forward()
     ag_forward(1)
     ag_start(3)
-    for copy in sendB:
-        copy.wait_recv()
+    ag_start(4)
     loads["cot"].wait()
     dy_start()
     h1_finish()
@@ -749,24 +753,30 @@
                 outs.append(mm(p.astype(BF16), v2))
             attQ[at_q, lanes(QC * r + 128 * j, 128)] = jnp.where(low, outs[0], outs[1]).astype(BF16)
 
-    loop(2 * S, lambda q: attend(2 * S * (1 - xx) + q))
+    def attend_pair(q):
+        attend(q)
+        attend(q + 1)
+
+    loop(S, lambda i: attend_pair(2 * S * (1 - xx) + 2 * i))
     go(needed)
     ag_forward(3)
-    loop(2 * S, lambda q: attend(2 * S * xx + q))
+    loop(S, lambda i: attend_pair(2 * S * xx + 2 * i))
     go(near_needed)
     go(near_rest)
-    ZR = R["ZR"]
+    ZR, FR = R["ZR"], R["FR"]
     if relays:
         for k, end in ((0, 0), (2, 3)):
 
             @pl.when(z == end)
             def _():
+                FR[k] = jnp.zeros((2, B, HF), BF16)
                 for unit in range(4):
                     ZR[unit, k] = jnp.zeros((B, FC), BF16)
 
     needed.wait_recv()
     go(passed)
     wo_forward()
+    over(early, 0).wait_recv()
     ag_forward(4)
     wo_finish()
     near_needed.wait_recv()
@@ -774,9 +784,16 @@
 
     x1, dx1, acc = R["x1"], R["dx1"], R["acc"]
 
+    wide = 256
+
+    def mix_sum(j):
+        cols = lanes(wide * j, wide)
+        x1[:, cols] = tok[:, cols].astype(F32) + mm(attQ[at(T * r, T), :], WO[:, cols])
+
+    loop(D // wide, mix_sum)
+
     def mix(i):
-        x = tok[at(step * i, step), :].astype(F32) + mm(attQ[at(T * r + step * i, step), :], WO[...])
-        x1[at(step * i, step), :] = x
+        x = x1[at(step * i, step), :]
         inv = lax.rsqrt(jnp.mean(x * x, axis=-1, keepdims=True) + EPSILON)
         h2Q[at(T * r + step * i, step), :] = (x * inv * GA[1:2, :]).astype(BF16)
 
@@ -795,19 +812,21 @@
     hid, dgdu = R["hid"], R["dgdu"]
 
     def ffn(half, role):
-        def body(i):
-            at_i = at(T * role + L * i, L)
-            both = mm(h2Q[at_i, :], WB[:, half * FC : (half + 1) * FC])
-            gate, up = both[:, 0:HF], both[:, HF:FC]
+        at_r = at(T * role, T)
+
+        def body(j):
+            to_gate = lanes(half * FC + wide * j, wide)
+            to_up = lanes(half * FC + HF + wide * j, wide)
+            gate, up = mm(h2Q[at_r, :], WB[:, to_gate]), mm(h2Q[at_r, :], WB[:, to_up])
             sigma = 1.0 / (1.0 + jnp.exp(-gate))
             silu = gate * sigma
-            hid[at_i, half * HF : (half + 1) * HF] = (silu * up).astype(BF16)
-            d_hidden = mm(dyQ[at_i, :], WC[half * HF : (half + 1) * HF, :], NT)
+            hid[at_r, lanes(half * HF + wide * j, wide)] = (silu * up).astype(BF16)
+            d_hidden = mm(dyQ[at_r, :], WC[at(half * HF + wide * j, wide), :], NT)
             d_gate = d_hidden * up * (sigma * (1.0 + gate * (1.0 - sigma)))
-            dgdu[at_i, half * FC : half * FC + HF] = d_gate.astype(BF16)
-            dgdu[at_i, half * FC + HF : (half + 1) * FC] = (d_hidden * silu).astype(BF16)
-
-        loop(T // L, body)
+            dgdu[at_r, to_gate] = d_gate.astype(BF16)
+            dgdu[at_r, to_up] = (d_hidden * silu).astype(BF16)
+
+        loop(HF // wide, body)
 
     ffn(0, r)
     ag_forward(7)
@@ -825,22 +844,29 @@
         at_g = lanes(B * group, B)
         if unit == 0:
             store(slice(0, FC), mm(hid[:, at_g], dyQ[...], TN))
-        elif unit < 3:
-            store(slice(0, FC), mm(h2Q[:, at_g], dgdu[:, (unit - 1) * FC : unit * FC], TN))
+        elif unit == 1:
+            store(slice(HF, FC), mm(h2Q[:, at_g], dgdu[:, HF:FC], TN))
+        elif unit == 2:
+            store(slice(0, FC), mm(h2Q[:, at_g], dgdu[:, FC : 2 * FC], TN))
         else:
             store(slice(0, 3 * QC), mm(h1Q[:, at_g], WC[:, 0 : 3 * QC], TN))
             store(slice(3 * QC, 4 * QC), mm(attQ[:, at_g], R["daR"][...], TN))
 
     slots = {1: 0, 2: 1, 0: 2, 3: 0}
 
+    def part(unit, ref):
+        return ref.at[:, pl.ds(HF, HF)] if unit == 1 else ref
+
     def y_copy(unit, i):
-        return remote(YS.at[slots[unit], i], YR.at[unit, i], peer, y_sem[unit] + i)
+        return remote(part(unit, YS.at[slots[unit], i]), part(unit, YR.at[unit, i]), peer, y_sem[unit] + i)
 
     def z_copy(unit, d, i=0):
-        return remote(YR.at[unit, i], ZR.at[unit, d - 1], z_dev(d), z_sem[unit] + d - 1)
+        return remote(part(unit, YR.at[unit, i]), part(unit, ZR.at[unit, d - 1]), z_dev(d), z_sem[unit] + d - 1)
+
+    middle = (1 + lax.div(z, 2)) * 8 + y * 4 + r
 
     def x_copy(unit, i=0):
-        return remote(YR.at[unit, i], ZX.at[unit], (1 + lax.div(z, 2)) * 8 + y * 4 + r, x_sem[unit])
+        return remote(part(unit, YR.at[unit, i]), part(unit, ZX.at[unit]), middle, x_sem[unit])
 
     def target(unit, i):
         if not relays:
@@ -895,11 +921,63 @@
             @pl.when(inner)
             def _():
                 x_copy(unit).wait_recv()
-                YR[unit, i] = (YR[unit, i].astype(F32) + ZX[unit].astype(F32)).astype(BF16)
+                cols = slice(HF if unit == 1 else 0, FC)
+                YR[unit, i, :, cols] = (YR[unit, i, :, cols].astype(F32) + ZX[unit, :, cols].astype(F32)).astype(BF16)
                 z_copy(unit, 2, i).start()
 
     def rs_second(unit, begin=0, count=Z):
         loop(count, lambda i: rs_step(unit, begin + i))
+
+    FS, FR, FX, FT, FK = (R[k] for k in ("FS", "FR", "FX", "FT", "FK"))
+    fz_sem, fx_sem = take(Z - 1), take()
+    last_over = remote(FT.at[0], FT.at[1], peer)
+
+    def zf_copy(d, i=0):
+        return remote(FS.at[i], FR.at[d - 1], z_dev(d), fz_sem + d - 1)
+
+    def zf_far(i=0):
+        return remote(FS.at[i], FX, middle, fx_sem)
+
+    def zf_first():
+        def body(i):
+            goal = target(1, i)
+            d = lax.rem(goal + Z - z, Z)
+            for side in range(2):
+                FS[i, side] = mm(h2Q[:, lanes(B * (2 * goal + side), B)], dgdu[:, 0:HF], TN).astype(BF16)
+            if not relays:
+                pl.when(d != 0)(lambda: zf_copy(d, i).start())
+                return
+            far = outer & (goal + z == 3)
+            pl.when(far)(lambda: zf_far(i).start())
+            pl.when((d != 0) & jnp.logical_not(far | (inner & (d == 2))))(lambda: zf_copy(d, i).start())
+
+        loop(Z, body)
+
+    def zf_relay():
+        if relays:
+
+            @pl.when(inner)
+            def _():
+                zf_far().wait_recv()
+                FS[3] = (FS[3].astype(F32) + FX[...].astype(F32)).astype(BF16)
+                zf_copy(2, 3).start()
+
+    def zf_second():
+        for d in range(1, Z):
+            if relays and d != 2:
+                pl.when(z != (0 if d == 1 else Z - 1))(zf_copy(d).wait_recv)
+            else:
+                zf_copy(d).wait_recv()
+
+        def total(side):
+            value = FS[own_place(1), side].astype(F32)
+            for d in range(1, Z):
+                value = value + FR[d - 1, side].astype(F32)
+            return value
+
+        FT[0] = total(1 - y).astype(BF16)
+        go(last_over)
+        FK[...] = total(y)
 
     quad_copies = {}
 
@@ -910,11 +988,16 @@
             else:
                 z_copy(unit, d).wait_recv()
         width = 256
+        if unit == 1:
+            last_over.wait_recv()
         for j in range(FC // width):
             cols = slice(width * j, width * (j + 1))
-            value = YR[unit, own_place(unit), :, cols].astype(F32)
-            for i in range(1, Z):
-                value = value + ZR[unit, i - 1, :, cols].astype(F32)
+            if unit == 1 and width * j < HF:
+                value = FK[:, cols] + FT[1, :, cols].astype(F32)
+            else:
+                value = YR[unit, own_place(unit), :, cols].astype(F32)
+                for i in range(1, Z):
+                    value = value + ZR[unit, i - 1, :, cols].astype(F32)
             if unit == 0:
                 R["gd"][:, cols] = value
             else:
@@ -933,8 +1016,6 @@
     rsS, rsR = R["rsS"], R["rsR"]
 
     def quad_sum(kind, prepare_block, partial, fill=None):
-        width = 512
-        tiles = [slice(width * j, width * (j + 1)) for j in range(D // width)]
         copies = [
             remote(rsS.at[0], rsR.at[kind, 0], sib),
             remote(rsS.at[1], rsR.at[kind, 1], sib),
@@ -942,23 +1023,22 @@
         ]
 
         def blocks(role, store):
-            def body(i):
-                for cols in tiles:
-                    store(at(L * i, L), cols, partial(at(T * role + L * i, L), cols))
-
-            loop(T // L, body)
-
-        def to_dia(at_i, cols, value):
-            rsS[1, at_i, cols] = value.astype(BF16)
-
-        def to_par(at_i, cols, value):
-            rsS[2, at_i, cols] = (value + rsR[kind, 1, at_i, cols].astype(F32)).astype(BF16)
-
-        def to_sib(at_i, cols, value):
-            rsS[0, at_i, cols] = value.astype(BF16)
-
-        def keep(at_i, cols, value):
-            acc[at_i, cols] = value
+            def body(j):
+                store(lanes(wide * j, wide), partial(at(T * role, T), wide * j))
+
+            loop(D // wide, body)
+
+        def to_dia(cols, value):
+            rsS[1, :, cols] = value.astype(BF16)
+
+        def to_par(cols, value):
+            rsS[2, :, cols] = (value + rsR[kind, 1, :, cols].astype(F32)).astype(BF16)
+
+        def to_sib(cols, value):
+            rsS[0, :, cols] = value.astype(BF16)
+
+        def keep(cols, value):
+            acc[:, cols] = value
 
         prepare_block(r_dia)
         blocks(r_dia, to_dia)
@@ -991,13 +1071,14 @@
     def nothing(role):
         return None
 
+    zf_first()
     rs_first(1)
     rs_first(0, 0, Z // 2)
     ag_finish(6)
     ag_finish(7)
     h2_sum = quad_sum(
-        0, functools.partial(ffn, 1), lambda at_i, cols: mm(dgdu[at_i, :], WB[cols, :], NT),
-        lambda i: rs_second(1, i, 1),
+        0, functools.partial(ffn, 1), lambda at_r, j: mm(dgdu[at_r, :], WB[at(j, wide), :], NT),
+        lambda i: (zf_relay() if i else None, rs_second(1, i, 1)),
     )
     rs_second(1, 2, 1)
     rs_first(2)
@@ -1024,11 +1105,10 @@
     sendD = [remote(daS.at[:, lanes(QC * q, QC)], daR.at[at(T * r, T)], dev) for dev, q in quad]
     sendT = [remote(dattS.at[:, lanes(QC * q, QC)], dattR.at[at(T * r, T)], dev) for dev, q in quad]
 
-    def out_back(i):
-        at_i = at(step * i, step)
-        dattS[at_i, :] = mm(daS[at_i, :], WO[...], NT).astype(BF16)
-
-    loop(T // step, out_back)
+    def out_back(j):
+        dattS[:, lanes(wide * j, wide)] = mm(daS[...], WO[at(wide * j, wide), :], NT).astype(BF16)
+
+    loop(D // wide, out_back)
     for copy in sendT:
         go(copy)
     for copy in sendD:
@@ -1037,9 +1117,10 @@
     daR[at(T * r, T), :] = daS[:, lanes(QC * r, QC)]
     rs_second(1, 3, 1)
     rs_first(0, Z // 2, Z // 2)
+    zf_second()
     rs_relay(1)
     rs_second(0, 0, Z // 2)
-    out_sum = quad_sum(1, nothing, lambda at_i, cols: mm(hid[at_i, :], WC[:, cols]))
+    out_sum = quad_sum(1, nothing, lambda at_r, j: mm(hid[at_r, :], WC[:, lanes(j, wide)]))
     ag_drain(2)
     ag_drain(3)
     for copy in sendT:
@@ -1104,7 +1185,7 @@
     out_sum()
     loop(T // step, write_out)
     in_sum = quad_sum(
-        2, nothing, lambda at_i, cols: mm(WC[at_i, 0 : 3 * QC], WA[cols, 0 : 3 * QC], NT),
+        2, nothing, lambda at_r, j: mm(WC[at_r, 0 : 3 * QC], WA[at(j, wide), 0 : 3 * QC], NT),
         lambda i: rs_second(0, Z // 2 + i, 1),
     )
     rs_relay(0)
@@ -1147,6 +1228,10 @@
     rs_last(3)
     for copy in sent:
         copy.wait_send()
+    for d in range(1, Z):
+        nearby(d, zf_copy(d).wait_send)
+    if relays:
+        pl.when(outer)(zf_far().wait_send)
     for unit in range(4):
         for i in range(Z):
             if unit != 1:

time: 229 us -> 211 us (0.921)
  Pallas kernels: 225 us -> 207 us
    pallas_call x1, Pallas kernels: 221 us -> 204 us  [layer(): pl.pallas_call(functools.partial(fused, s, names), out_shape=[tokens_shap...]
where the time goes in v5:
time: 211 us
  Pallas kernels  207 us (98%)
    pallas_call x1, Pallas kernels, layer(): pl.pallas_call(functools.partial(fused, s, names), out_shape=[tokens_shap...  204 us

profile of v5, /device:TPU:25, one launch (start us, length us, event | category | flops | bytes accessed | tf_op | source)
XLA Modules:
  0.0 210.6 jit_solution(18233647735094110327)
XLA Ops:
  0.6 0.0 copy-start.3
  0.7 0.6 copy-done.3
  1.3 0.0 copy-start.4
  1.3 0.1 convert_element_type.52
  1.4 0.6 copy-done.4
  2.0 0.0 copy-start
  2.0 0.0 copy-start.1
  2.0 0.0 copy-start.2
  2.0 0.1 convert_element_type.54
  2.1 0.6 copy-done
  2.6 0.0 copy-done.1
  2.6 0.0 copy-done.2
  2.6 0.6 convert_add_fusion.refs_12_
  3.3 203.9 %fused_layer.1 = (bf16[256,1024]{1,0:T(8,128)(2,1)}, bf16[256,1024]{1,0:T(8,128)(2,1)}, f32[128,1024]{1,0:T(8,128)}, bf16[3,4,32,1024]{3,2,1,0:T(8,128)(2,1)}, f32[8,1024]{1,0:T(8,128)}) custom-call(bf16[256,1024]{1,0:T(8,128)(2,1)} %bitcast.10, bf16[256,1024]{1,0:T(8,128)(2,1)} %bitcast.11, s32[2,128]{1,0:T(2,128)} %refs_2_.1, s32[2,128]{1,0:T(2,128)} %refs_3_.1, ...), custom_call_target="tpu_custom_call" | custom-call | tf_op jit(solution)/shard_map/fused_layer/pallas_call | solution.py:1297
  207.1 3.3 %finishing.1 = (bf16[256,1024]{1,0:T(8,128)(2,1)}, bf16[256,1024]{1,0:T(8,128)(2,1)}, f32[32,1024]{1,0:T(8,128)}, f32[32,1024]{1,0:T(8,128)}, f32[32,1024]{1,0:T...) custom-call(bf16[256,1024]{1,0:T(8,128)(2,1)} %get-tuple-element.33., ...), custom_call_target="tpu_custom_call" | custom-call | tf_op jit(solution)/shard_map/finishing/pallas_call | solution.py:1311
  (2 shorter events, 0.0 us)
Async XLA Ops:
  0.6 0.7 copy-start.3
  1.3 0.7 copy-start.4
  2.0 0.7 copy-start
  2.0 0.7 copy-start.1
  2.0 0.7 copy-start.2

commit v6 on v5

--- a/solution.py
+++ b/solution.py
@@ -524,7 +524,7 @@
 
     chunks = [(WA, 0, 2 * QC), (WA, 2 * QC, 2 * QC), (WC, 0, D // 2), (WC, D // 2, D // 2)]
     chunks += [(WB, HF * k, HF) for k in range(4)] + [(GA, 0, B)]
-    early, after = 7, {0: 2, 1: 3, 2: 4, 3: 5, 4: 6}
+    early, after = 7, {1: 4, 2: 5, 3: 6}
 
     def piece(k, group):
         ref, start, size = chunks[k]
@@ -605,6 +605,9 @@
     for copy in sendG + sendA + sendI:
         go(copy)
     loads["wd"].wait()
+    ag_own(2)
+    ag_own(3)
+    ag_start(2)
     for copy in sendG:
         copy.wait_recv()
     GA[:, lanes(B * g, B)] = (GQ[0] + GQ[1]) + (GQ[2] + GQ[3])
@@ -680,10 +683,9 @@
         copy.wait_recv()
     ag_own(early)
     ag_forward(0)
-    ag_start(2)
+    ag_start(3)
     h1_forward()
     ag_forward(1)
-    ag_start(3)
     ag_start(4)
     loads["cot"].wait()
     dy_start()

time: 211 us -> 208 us (0.986)
  Pallas kernels: 207 us -> 204 us
    pallas_call x1, Pallas kernels: 204 us -> 201 us  [layer(): pl.pallas_call(functools.partial(fused, s, names), out_shape=[tokens_shap...]
where the time goes in v6:
time: 208 us
  Pallas kernels  204 us (98%)
    pallas_call x1, Pallas kernels, layer(): pl.pallas_call(functools.partial(fused, s, names), out_shape=[tokens_shap...  201 us

profile of v6, /device:TPU:25, one launch (start us, length us, event | category | flops | bytes accessed | tf_op | source)
XLA Modules:
  0.0 207.9 jit_solution(17063529173243371491)
XLA Ops:
  0.6 0.0 copy-start.3
  0.7 0.6 copy-done.3
  1.3 0.0 copy-start.4
  1.3 0.1 convert_element_type.52
  1.4 0.6 copy-done.4
  2.0 0.0 copy-start
  2.0 0.0 copy-start.1
  2.0 0.0 copy-start.2
  2.0 0.1 convert_element_type.54
  2.1 0.6 copy-done
  2.6 0.0 copy-done.1
  2.6 0.0 copy-done.2
  2.6 0.6 convert_add_fusion.refs_12_
  3.3 201.1 %fused_layer.1 = (bf16[256,1024]{1,0:T(8,128)(2,1)}, bf16[256,1024]{1,0:T(8,128)(2,1)}, f32[128,1024]{1,0:T(8,128)}, bf16[3,4,32,1024]{3,2,1,0:T(8,128)(2,1)}, f32[8,1024]{1,0:T(8,128)}) custom-call(bf16[256,1024]{1,0:T(8,128)(2,1)} %bitcast.10, bf16[256,1024]{1,0:T(8,128)(2,1)} %bitcast.11, s32[2,128]{1,0:T(2,128)} %refs_2_.1, s32[2,128]{1,0:T(2,128)} %refs_3_.1, ...), custom_call_target="tpu_custom_call" | custom-call | tf_op jit(solution)/shard_map/fused_layer/pallas_call | solution.py:1299
  204.4 3.3 %finishing.1 = (bf16[256,1024]{1,0:T(8,128)(2,1)}, bf16[256,1024]{1,0:T(8,128)(2,1)}, f32[32,1024]{1,0:T(8,128)}, f32[32,1024]{1,0:T(8,128)}, f32[32,1024]{1,0:T...) custom-call(bf16[256,1024]{1,0:T(8,128)(2,1)} %get-tuple-element.33., ...), custom_call_target="tpu_custom_call" | custom-call | tf_op jit(solution)/shard_map/finishing/pallas_call | solution.py:1313
  (2 shorter events, 0.0 us)
Async XLA Ops:
  0.6 0.7 copy-start.3
  1.3 0.7 copy-start.4
  2.0 0.7 copy-start
  2.0 0.7 copy-start.1
  2.0 0.7 copy-start.2

commit v7 on v6

--- a/solution.py
+++ b/solution.py
@@ -1121,7 +1121,6 @@
     rs_first(0, Z // 2, Z // 2)
     zf_second()
     rs_relay(1)
-    rs_second(0, 0, Z // 2)
     out_sum = quad_sum(1, nothing, lambda at_r, j: mm(hid[at_r, :], WC[:, lanes(j, wide)]))
     ag_drain(2)
     ag_drain(3)
@@ -1179,6 +1178,7 @@
             attend_back(S * i + q)
         rs_step(2, i)
 
+    rs_second(0, 0, Z // 2)
     loop(4, attend_and_step)
     for copy in sendD + [near_rest, passed_rest]:
         copy.wait_recv()
@@ -1216,8 +1216,9 @@
         TT[0, 3 + m : 4 + m, 0:128] = line
     t1, t2, t3, t_finish = tile_sum(TT, TR)
     t1()
-    rs_second(3, 0, 3)
+    rs_second(3, 0, 2)
     t2()
+    rs_second(3, 2, 1)
     rs_second(3, 3, 1)
     rs_relay(3)
     rs_third(2)

time: 208 us -> 212 us (1.019)
  Pallas kernels: 204 us -> 207 us
    pallas_call x1, Pallas kernels: 201 us -> 203 us  [layer(): pl.pallas_call(functools.partial(fused, s, names), out_shape=[tokens_shap...]
where the time goes in v7:
time: 212 us; the launch traced here: 210 us
  Pallas kernels  207 us (98%)
    pallas_call x1, Pallas kernels, layer(): pl.pallas_call(functools.partial(fused, s, names), out_shape=[tokens_shap...  203 us

profile of v7, /device:TPU:25, one launch (start us, length us, event | category | flops | bytes accessed | tf_op | source)
XLA Modules:
  0.0 210.1 jit_solution(11111724075953158968)
XLA Ops:
  0.6 0.0 copy-start.3
  0.7 0.6 copy-done.3
  1.3 0.0 copy-start.4
  1.3 0.1 convert_element_type.52
  1.4 0.6 copy-done.4
  2.0 0.0 copy-start
  2.0 0.0 copy-start.1
  2.0 0.0 copy-start.2
  2.0 0.1 convert_element_type.54
  2.1 0.6 copy-done
  2.6 0.0 copy-done.1
  2.6 0.0 copy-done.2
  2.6 0.6 convert_add_fusion.refs_12_
  3.3 203.3 %fused_layer.1 = (bf16[256,1024]{1,0:T(8,128)(2,1)}, bf16[256,1024]{1,0:T(8,128)(2,1)}, f32[128,1024]{1,0:T(8,128)}, bf16[3,4,32,1024]{3,2,1,0:T(8,128)(2,1)}, f32[8,1024]{1,0:T(8,128)}) custom-call(bf16[256,1024]{1,0:T(8,128)(2,1)} %bitcast.10, bf16[256,1024]{1,0:T(8,128)(2,1)} %bitcast.11, s32[2,128]{1,0:T(2,128)} %refs_2_.1, s32[2,128]{1,0:T(2,128)} %refs_3_.1, ...), custom_call_target="tpu_custom_call" | custom-call | tf_op jit(solution)/shard_map/fused_layer/pallas_call | solution.py:1300
  206.6 3.3 %finishing.1 = (bf16[256,1024]{1,0:T(8,128)(2,1)}, bf16[256,1024]{1,0:T(8,128)(2,1)}, f32[32,1024]{1,0:T(8,128)}, f32[32,1024]{1,0:T(8,128)}, f32[32,1024]{1,0:T...) custom-call(bf16[256,1024]{1,0:T(8,128)(2,1)} %get-tuple-element.33., ...), custom_call_target="tpu_custom_call" | custom-call | tf_op jit(solution)/shard_map/finishing/pallas_call | solution.py:1314
  (2 shorter events, 0.0 us)
Async XLA Ops:
  0.6 0.7 copy-start.3
  1.3 0.7 copy-start.4
  2.0 0.7 copy-start
  2.0 0.7 copy-start.1
  2.0 0.7 copy-start.2
